TPU v7x, 128 devices: a whole 4x4x4 slice. The times are simulated.
128 devices in a mesh: set: 4 (over x), sub: 32 (over z, y, core).
Axes of the slice: x: 4, y: 4, z: 4, core: 2. Of those that a mesh axis runs over, the one named last changes fastest.
Arguments:
- jump_rhs: float32 [32, 1048576], P(None, ('set', 'sub')), may hold values from -21 to 21
- w_factor: bfloat16 [2048, 512, 512], P(('set', 'sub')), may hold values from -1 to 7
- s_factor: bfloat16 [2048, 512, 512], P(('set', 'sub')), may hold values from -1 to 7
- rigid_coarse_blocks: float32 [2048, 6, 512], P(('set', 'sub')), may hold values from -0.5 to 0.5
- coarse_factor: float32 [2048, 512], P('set'), may hold values from -1 to 5
- slot_of_row: int32 [1048576], P(('set', 'sub')), may hold values from 0 to 8191, as said below
- pair_counts: int32 [128, 32], P(('set', 'sub')), may hold values from 128 to 256, as said below
- corner_map: int32 [2048, 6], P(('set', 'sub')), may hold values from 0 to 511
Outputs:
- multipliers: float32 [32, 1048576], P(None, ('set', 'sub'))
- residual: float32 [32, 1048576], P(None, ('set', 'sub'))
Inputs may be any that keep to these rules, and one draw needn't show every extreme that they name: `slot_of_row`: on each device the 8192 entries are a permutation of 0 to 8191; write a slot as j * 256 + i. On device d of a set (d its sub index) the row in slot j * 256 + i is paired with the row in slot d * 256 + i of device j of the same set when j != d, and with the row in slot d * 256 + (i xor 1) of device d itself when j == d. Slot j * 256 + i of device d is live exactly when i < pair_counts[d, j]. Within a set the table is symmetric in d and j, its diagonal is even, and some entry of every set equals 256.
All inputs are finite; a program needn't handle non-finite values.
Results may differ from a plain program's by a relative error of at most 0.0056.
Values sent between devices are 32-bit elements; how exact they have to be, the bound alone decides.
A program may use at most 192 MiB of HBM per device.

v0:
```python
import jax
import jax.numpy as jnp
from jax import lax
from jax.sharding import PartitionSpec as P

ITERS = 2


highest_accuracy = lax.Precision.HIGHEST


def body(
    jump_rhs,
    w_factor,
    s_factor,
    rigid_coarse_blocks,
    coarse_factor,
    slot_of_row,
    pair_counts,
    corner_map,
):
    load_count, dev_rows = jump_rhs.shape
    sub_count, sub_rows, _ = w_factor.shape
    mode_count = rigid_coarse_blocks.shape[1]
    coarse_dim = coarse_factor.shape[0]
    peer_count = lax.axis_size("sub")
    slot_cap = dev_rows // peer_count
    my_index = lax.axis_index("sub")
    flat = jnp.arange(dev_rows, dtype=jnp.int32)
    row_of_slot = jnp.zeros((dev_rows,), jnp.int32).at[slot_of_row].set(flat)
    own_block = flat // slot_cap == my_index
    live = (flat % slot_cap < pair_counts[0][flat // slot_cap]).astype(jnp.float32)

    def to_rows(vector):
        return vector[:, slot_of_row]

    def to_slots(vector):
        return vector[:, row_of_slot]

    def finish_pairs(received):
        received = received.reshape(load_count, dev_rows)
        swapped = received.reshape(load_count, dev_rows // 2, 2)[:, :, ::-1].reshape(
            load_count, dev_rows
        )
        return jnp.where(own_block[None, :], swapped, received)

    def apply_factor(vector, cholesky_factor):
        rounded_values = vector.astype(jnp.bfloat16).reshape(load_count, sub_count, sub_rows)
        half_product = jnp.einsum(
            "muq,uqg->mug", rounded_values, cholesky_factor, preferred_element_type=jnp.float32
        ).astype(jnp.bfloat16)
        final_output = jnp.einsum(
            "gzf,zbf->gzb", half_product, cholesky_factor, preferred_element_type=jnp.float32
        )
        return final_output.reshape(load_count, dev_rows)

    corner_flat = corner_map.reshape(-1)
    coarse_ids = jnp.arange(coarse_dim, dtype=jnp.int32)
    local_onehot = (corner_flat[:, None] == coarse_ids[None, :]).astype(jnp.float32)
    all_corners = lax.all_gather(corner_flat, "sub", axis=0, tiled=True)
    full_onehot = (all_corners[:, None] == coarse_ids[None, :]).astype(jnp.float32)

    def precondition(residual):
        shaped = residual.reshape(load_count, peer_count, slot_cap)
        paired = live * (
            residual
            + finish_pairs(lax.all_to_all(shaped, "sub", split_axis=1, concat_axis=1, tiled=True))
        )
        flexed = to_slots(apply_factor(to_rows(paired), s_factor))
        shaped_flex = flexed.reshape(load_count, peer_count, slot_cap)
        return live * (
            flexed
            + finish_pairs(
                lax.all_to_all(shaped_flex, "sub", split_axis=1, concat_axis=1, tiled=True)
            )
        )

    def energy_of(residual, precond):
        return lax.psum(jnp.sum(residual * precond, axis=1), ("set", "sub"))

    residual = live * to_slots(jump_rhs)
    multipliers = jnp.zeros((load_count, dev_rows), jnp.float32)
    precond = precondition(residual)
    energy = energy_of(residual, precond)
    direction = precond
    for turn_index in range(ITERS):
        direction_rows = to_rows(direction)
        shaped_dir = direction.reshape(load_count, peer_count, slot_cap)
        paired_dir = live * (
            direction
            + finish_pairs(
                lax.all_to_all(shaped_dir, "sub", split_axis=1, concat_axis=1, tiled=True)
            )
        )
        paired_rows = to_rows(paired_dir)
        flexed_rows = apply_factor(paired_rows, w_factor)
        reshaped_rows = direction_rows.reshape(load_count, sub_count, sub_rows)
        local_coarse_part = jnp.einsum(
            "ejn,jbn->ejb", reshaped_rows, rigid_coarse_blocks, precision=highest_accuracy
        )
        local_coarse_part = local_coarse_part.reshape(load_count, sub_count * mode_count)
        gathered = lax.all_gather(local_coarse_part, "sub", axis=1, tiled=True)
        coarse_in = jnp.dot(gathered, full_onehot, precision=highest_accuracy)
        middle = jnp.dot(coarse_in, coarse_factor, precision=highest_accuracy)
        coarse_sol = jnp.dot(middle, coarse_factor.T, precision=highest_accuracy)
        coarse_back_solve = jnp.dot(coarse_sol, local_onehot.T, precision=highest_accuracy)
        back_solve = jnp.einsum(
            "tbv,bvu->tbu",
            coarse_back_solve.reshape(load_count, sub_count, mode_count),
            rigid_coarse_blocks,
            precision=highest_accuracy,
        )
        coarse_rows, local_coarse_part, coarse_back_solve = (
            back_solve.reshape(load_count, dev_rows),
            local_coarse_part,
            coarse_back_solve,
        )
        flexed = to_slots(flexed_rows)
        coarse_part = live * to_slots(coarse_rows)
        shaped_img = flexed.reshape(load_count, peer_count, slot_cap)
        image = (
            live
            * (
                flexed
                + finish_pairs(
                    lax.all_to_all(shaped_img, "sub", split_axis=1, concat_axis=1, tiled=True)
                )
            )
            + coarse_part
        )
        curvature = lax.psum(jnp.sum(direction * image, axis=1), ("set", "sub"))
        step_alpha = energy / curvature
        multipliers = multipliers + step_alpha[:, None] * direction
        residual = residual - step_alpha[:, None] * image
        if turn_index + 1 < ITERS:
            precond = precondition(residual)
            new_energy = energy_of(residual, precond)
            direction = precond + (new_energy / energy)[:, None] * direction
            energy = new_energy
    return (to_rows(multipliers), to_rows(residual))


def solution(mesh):
    return jax.shard_map(
        body,
        mesh=mesh,
        in_specs=(
            P(None, ("set", "sub")),
            P(("set", "sub"), None, None),
            P(("set", "sub"), None, None),
            P(("set", "sub"), None, None),
            P("set", None),
            P(("set", "sub")),
            P(("set", "sub"), None),
            P(("set", "sub"), None),
        ),
        out_specs=(P(None, ("set", "sub")), P(None, ("set", "sub"))),
        check_vma=False,
    )
```

profile of v0, /device:TPU:1, one launch (start us, length us, event | category | flops | bytes accessed | tf_op | source)
XLA Modules:
  0.0 1501.3 jit_solution(14180607669639555938)
XLA Ops:
  6.0 4.5 compare_select_fusion.1
  10.5 15.7 %fusion.73 = (f32[8192]{0:T(1024)S(1)}, s32[8192]{0:T(1024)S(1)}) fusion(pred[8192]{0:T(1024)(128)(4,1)S(1)} %compare_reduce_fusion, pred[8192]{0:T(1024)(128)(4,1)S(1)} %compare_reduce_fusion.1, pred[8192]{0:T(1024)(128)(4,1)S(1)} %compare_reduce_fusion.2, pred[8192]{0:T(1024)(128)(4,1)S(1)} %compare_reduce_fusion.3, ...), kind=kLoop, calls=%fused_computation.176 | loop fusion | flops 270336 | bytes 303204 | tf_op jit(solution)/shard_map/convert_element_type | solution.py:32
  27.0 30.5 %scatter_custom_fusion = s32[8192]{0:T(1024)S(1)} fusion(s32[8192]{0:T(1024)S(1)} %get-tuple-element.25, s32[8192]{0:T(1024)S(1)} %iota.87, s32[]{:T(128)} %constant.46.clone.1), kind=kCustom, calls=%fused_computation.179 | custom fusion | bytes 32772 | tf_op jit(solution)/shard_map/scatter | solution.py:30
  61.1 29.9 %gather_fusion = f32[8192,32]{1,0:T(8,128)} fusion(f32[32,8192]{0,1:T(8,128)} %copy.93, s32[8192]{0:T(1024)S(1)} %fusion.63), kind=kCustom, calls=%fused_computation | custom fusion | bytes 2129920 | tf_op jit(solution)/shard_map/gather | solution.py:38
  91.0 4.1 broadcast_multiply_fusion
  98.7 9.6 all-to-all-start
  108.4 17.2 %all-to-all-done = f32[32,32,256]{2,0,1:T(8,128)S(1)} async-done(((f32[32,32,256]{2,0,1:T(8,128)}), f32[32,32,256]{2,0,1:T(8,128)S(1)}, u32[]{:S(2)}, u32[]{:S(2)}) %all-to-all-start) | async-done | bytes 1048608 | tf_op jit(solution)/shard_map/all_to_all | solution.py:67
  128.1 20.6 %rev.24 = f32[32,4096,2]{0,2,1:T(2,128)} reverse(f32[32,4096,2]{0,2,1:T(2,128)} %bitcast.334), dimensions={2} | reverse | bytes 2097152 | tf_op jit(solution)/shard_map/rev | solution.py:42
  148.7 7.6 fusion.34
  156.3 29.2 %gather_fusion.1 = bf16[8192,32]{1,0:T(8,128)(2,1)} fusion(bf16[32,8192]{0,1:T(8,128)(2,1)S(1)} %fusion.34, s32[8192]{0:T(1024)S(1)} %get-tuple-element.24), kind=kCustom, calls=%fused_computation.1 | custom fusion | bytes 1081344 | tf_op jit(solution)/shard_map/gather | solution.py:35
  185.6 10.3 convolution_bitcast_fusion.5
  198.5 29.9 %gather_fusion.2 = f32[8192,32]{1,0:T(8,128)} fusion(f32[32,8192]{0,1:T(8,128)} %bitcast.336, s32[8192]{0:T(1024)S(1)} %fusion.63), kind=kCustom, calls=%fused_computation.2 | custom fusion | bytes 2129920 | tf_op jit(solution)/shard_map/gather | solution.py:38
  232.0 4.0 all-to-all-start.1
  237.7 15.5 %all-to-all-done.1 = f32[32,32,256]{2,0,1:T(8,128)S(1)} async-done(((f32[32,32,256]{2,0,1:T(8,128)}), f32[32,32,256]{2,0,1:T(8,128)S(1)}, u32[]{:S(2)}, u32[]{:S(2)}) %all-to-all-start.1) | async-done | bytes 1048608 | tf_op jit(solution)/shard_map/all_to_all | solution.py:74
  255.9 20.5 %rev.25 = f32[32,4096,2]{0,2,1:T(2,128)} reverse(f32[32,4096,2]{0,2,1:T(2,128)} %bitcast.311), dimensions={2} | reverse | bytes 2097152 | tf_op jit(solution)/shard_map/rev | solution.py:42
  276.5 9.4 fusion.30
  289.5 4.6 all-to-all-start.2
  294.1 127.3 %all-reduce = s32[3072]{0:T(1024)} all-reduce(s32[3072]{0:T(1024)S(1)} %dynamic-update-slice), channel_id=1, replica_groups=mesh['set'=4,'sub'=32] {'sub'}, use_global_device_ids=true, to_apply=%add | all-reduce | flops 3072 | bytes 24576
  424.8 4.4 fusion.39
  432.8 20.6 %rev.26 = f32[32,4096,2]{0,2,1:T(2,128)} reverse(f32[32,4096,2]{0,2,1:T(2,128)} %bitcast.332), dimensions={2} | reverse | bytes 2097152 | tf_op jit(solution)/shard_map/rev | solution.py:42
  453.4 12.4 fusion.28
  465.8 29.9 %gather_fusion.3 = bf16[8192,32]{1,0:T(8,128)(2,1)} fusion(bf16[32,8192]{0,1:T(8,128)(2,1)} %get-tuple-element.20, s32[8192]{0:T(1024)S(1)} %get-tuple-element.24), kind=kCustom, calls=%fused_computation.3 | custom fusion | bytes 1081344 | tf_op jit(solution)/shard_map/gather | solution.py:35
  495.7 11.3 convolution_bitcast_fusion.4
  510.6 29.9 %gather_fusion.4 = f32[8192,32]{1,0:T(8,128)} fusion(f32[32,8192]{0,1:T(8,128)} %bitcast.337, s32[8192]{0:T(1024)S(1)} %fusion.63), kind=kCustom, calls=%fused_computation.4 | custom fusion | bytes 2129920 | tf_op jit(solution)/shard_map/gather | solution.py:38
  544.1 9.9 all-to-all-start.3
  554.0 29.9 %gather_fusion.5 = f32[8192,32]{1,0:T(8,128)} fusion(f32[32,8192]{0,1:T(8,128)} %get-tuple-element.21, s32[8192]{0:T(1024)S(1)} %get-tuple-element.24), kind=kCustom, calls=%fused_computation.5 | custom fusion | bytes 2129920 | tf_op jit(solution)/shard_map/gather | solution.py:35
  583.9 4.1 convolution_bitcast_fusion.7
  589.5 25.7 %all-gather = f32[32,96,32]{1,2,0:T(8,128)S(1)} all-gather(f32[1,96,32]{1,2,0:T(8,128)S(1)} %copy.114), channel_id=1, replica_groups=mesh['set'=4,'sub'=32] {'sub'}, dimensions={0}, use_global_device_ids=true | all-gather | bytes 405504 | tf_op jit(solution)/shard_map/all_gather | solution.py:102
  630.8 29.9 %gather_fusion.6 = f32[8192,32]{1,0:T(8,128)} fusion(f32[32,8192]{0,1:T(8,128)} %bitcast.338, s32[8192]{0:T(1024)S(1)} %fusion.63), kind=kCustom, calls=%fused_computation.6 | custom fusion | bytes 2129920 | tf_op jit(solution)/shard_map/gather | solution.py:38
  660.7 3.7 copy.111
  664.4 20.5 %rev.27 = f32[32,4096,2]{0,2,1:T(2,128)} reverse(f32[32,4096,2]{0,2,1:T(2,128)} %bitcast.309), dimensions={2} | reverse | bytes 2097152 | tf_op jit(solution)/shard_map/rev | solution.py:42
  684.9 28.9 %multiply_reduce_fusion.1 = (f32[32]{0:T(128)S(1)}, f32[32]{0:T(128)S(1)}, f32[32,4096,2]{0,2,1:T(2,128)}, f32[32,4096,2]{0,2,1:T(2,128)}) fusion(f32[32,4096,2]{0,2,1:T(2,128)} %bitcast.299, f32[4096,2]{1,0:T(8,128)S(1)} %get-tuple-element.61, f32[32,4096,2]{0,2,1:T(2,128)} %bitcast.327, f32[32,4096,2]{0,2,1:T(2,128)} %bitcast.316, f32[32,4096,2]{0,2,1:T(2,128)} %rev.27, ...), kind=kLoop, calls=%fused_computation.70 | loop fusion | flops 3145664 | bytes 10526976 | tf_op jit(solution)/shard_map/reduce_sum | solution.py:131
  713.8 64.2 %all-reduce.1 = (f32[32]{0:T(128)S(1)}, f32[32]{0:T(128)S(1)}) all-reduce(f32[32]{0:T(128)S(1)} %get-tuple-element.11, f32[32]{0:T(128)S(1)} %get-tuple-element.10), channel_id=1, replica_groups=mesh['set'=4,'sub'=32] {'set','sub'}, use_global_device_ids=true, to_apply=%region_2.3 | all-reduce | flops 64 | bytes 512 | tf_op jit(solution)/shard_map/psum | solution.py:79
  778.0 10.5 fusion.21
  792.1 22.8 %all_to_all.40 = f32[32,32,256]{2,0,1:T(8,128)} all-to-all(f32[32,32,256]{2,0,1:T(8,128)} %copy.123), channel_id=1, replica_groups=mesh['set'=4,'sub'=32] {'sub'}, dimensions={1} | all-to-all | bytes 2097152 | tf_op jit(solution)/shard_map/all_to_all | solution.py:67
  818.5 20.5 %rev.28 = f32[32,4096,2]{0,2,1:T(2,128)} reverse(f32[32,4096,2]{0,2,1:T(2,128)} %bitcast.331), dimensions={2} | reverse | bytes 2097152 | tf_op jit(solution)/shard_map/rev | solution.py:42
  839.1 14.5 fusion.16
  853.6 29.8 %gather_fusion.7 = bf16[8192,32]{1,0:T(8,128)(2,1)} fusion(bf16[32,8192]{0,1:T(8,128)(2,1)} %get-tuple-element.16, s32[8192]{0:T(1024)S(1)} %get-tuple-element.24), kind=kCustom, calls=%fused_computation.7 | custom fusion | bytes 1081344 | tf_op jit(solution)/shard_map/gather | solution.py:35
  883.4 11.3 convolution_bitcast_fusion.2
  894.7 3.7 copy.163
  898.4 29.9 %gather_fusion.8 = f32[8192,32]{1,0:T(8,128)} fusion(f32[32,8192]{0,1:T(8,128)} %bitcast.339, s32[8192]{0:T(1024)S(1)} %fusion.63), kind=kCustom, calls=%fused_computation.8 | custom fusion | bytes 2129920 | tf_op jit(solution)/shard_map/gather | solution.py:38
  931.8 22.0 %all_to_all.41 = f32[32,32,256]{2,0,1:T(8,128)} all-to-all(f32[32,32,256]{2,0,1:T(8,128)} %copy.129), channel_id=1, replica_groups=mesh['set'=4,'sub'=32] {'sub'}, dimensions={1} | all-to-all | bytes 2097152 | tf_op jit(solution)/shard_map/all_to_all | solution.py:74
  957.4 20.6 %rev.29 = f32[32,4096,2]{0,2,1:T(2,128)} reverse(f32[32,4096,2]{0,2,1:T(2,128)} %bitcast.302), dimensions={2} | reverse | bytes 2097152 | tf_op jit(solution)/shard_map/rev | solution.py:42
  978.0 13.6 multiply_reduce_fusion
  991.6 63.6 %psum.30 = f32[32]{0:T(128)S(1)} all-reduce(f32[32]{0:T(128)S(1)} %multiply_reduce_fusion), channel_id=1, replica_groups=mesh['set'=4,'sub'=32] {'set','sub'}, use_global_device_ids=true, to_apply=%region_6.7 | all-reduce | flops 32 | bytes 256 | tf_op jit(solution)/shard_map/psum | solution.py:79
  1055.2 8.7 fusion.11
  1067.5 22.7 %all_to_all.42 = f32[32,32,256]{2,0,1:T(8,128)} all-to-all(f32[32,32,256]{2,0,1:T(8,128)} %copy.133), channel_id=1, replica_groups=mesh['set'=4,'sub'=32] {'sub'}, dimensions={1} | all-to-all | bytes 2097152 | tf_op jit(solution)/shard_map/all_to_all | solution.py:92
  1090.2 3.6 copy.134
  1093.8 20.5 %rev.30 = f32[32,4096,2]{0,2,1:T(2,128)} reverse(f32[32,4096,2]{0,2,1:T(2,128)} %bitcast.333), dimensions={2} | reverse | bytes 2097152 | tf_op jit(solution)/shard_map/rev | solution.py:42
  1114.4 13.7 fusion.8
  1128.0 29.8 %gather_fusion.9 = bf16[8192,32]{1,0:T(8,128)(2,1)} fusion(bf16[32,8192]{0,1:T(8,128)(2,1)} %get-tuple-element.14, s32[8192]{0:T(1024)S(1)} %get-tuple-element.24), kind=kCustom, calls=%fused_computation.9 | custom fusion | bytes 1081344 | tf_op jit(solution)/shard_map/gather | solution.py:35
  1157.9 11.3 convolution_bitcast_fusion.1
  1172.8 29.9 %gather_fusion.10 = f32[8192,32]{1,0:T(8,128)} fusion(f32[32,8192]{0,1:T(8,128)} %bitcast.340, s32[8192]{0:T(1024)S(1)} %fusion.63), kind=kCustom, calls=%fused_computation.10 | custom fusion | bytes 2129920 | tf_op jit(solution)/shard_map/gather | solution.py:38
  1206.3 4.6 all-to-all-start.7
  1210.9 29.9 %gather_fusion.11 = f32[8192,32]{1,0:T(8,128)} fusion(f32[32,8192]{0,1:T(8,128)} %get-tuple-element.15, s32[8192]{0:T(1024)S(1)} %get-tuple-element.24), kind=kCustom, calls=%fused_computation.11 | custom fusion | bytes 2129920 | tf_op jit(solution)/shard_map/gather | solution.py:35
  1240.8 4.1 convolution_bitcast_fusion.6
  1246.4 25.5 %all-gather.1 = f32[32,96,32]{1,2,0:T(8,128)S(1)} all-gather(f32[1,96,32]{1,2,0:T(8,128)S(1)} %copy.143), channel_id=1, replica_groups=mesh['set'=4,'sub'=32] {'sub'}, dimensions={0}, use_global_device_ids=true | all-gather | bytes 405504 | tf_op jit(solution)/shard_map/all_gather | solution.py:102
  1287.5 29.9 %gather_fusion.12 = f32[8192,32]{1,0:T(8,128)} fusion(f32[32,8192]{0,1:T(8,128)} %bitcast.335, s32[8192]{0:T(1024)S(1)} %fusion.63), kind=kCustom, calls=%fused_computation.12 | custom fusion | bytes 2129920 | tf_op jit(solution)/shard_map/gather | solution.py:38
  1321.0 20.5 %rev.31 = f32[32,4096,2]{0,2,1:T(2,128)} reverse(f32[32,4096,2]{0,2,1:T(2,128)} %bitcast.325), dimensions={2} | reverse | bytes 2097152 | tf_op jit(solution)/shard_map/rev | solution.py:42
  1341.5 14.7 fusion.35
  1356.2 63.8 %psum.31 = f32[32]{0:T(128)S(1)} all-reduce(f32[32]{0:T(128)S(1)} %fusion.35), channel_id=1, replica_groups=mesh['set'=4,'sub'=32] {'set','sub'}, use_global_device_ids=true, to_apply=%region_8.9 | all-reduce | flops 32 | bytes 256 | tf_op jit(solution)/shard_map/psum | solution.py:131
  1420.0 13.8 fusion.6
  1433.8 29.9 %gather_fusion.14 = f32[8192,32]{1,0:T(8,128)} fusion(f32[32,8192]{0,1:T(8,128)} %get-tuple-element.26, s32[8192]{0:T(1024)S(1)} %get-tuple-element.24), kind=kCustom, calls=%fused_computation.14 | custom fusion | bytes 2129920 | tf_op jit(solution)/shard_map/gather | solution.py:35
  1463.7 29.9 %gather_fusion.13 = f32[8192,32]{1,0:T(8,128)} fusion(f32[32,8192]{0,1:T(8,128)} %get-tuple-element.27, s32[8192]{0:T(1024)S(1)} %get-tuple-element.24), kind=kCustom, calls=%fused_computation.13 | custom fusion | bytes 2129920 | tf_op jit(solution)/shard_map/gather | solution.py:35
  (116 shorter events, 114.0 us)
Async XLA Ops:
  0.6 621.1 %copy-start = (f32[512,512]{1,0:T(8,128)S(1)}, f32[512,512]{1,0:T(8,128)}, u32[]{:S(2)}) copy-start(f32[512,512]{1,0:T(8,128)} %param.12) | copy-start | bytes 3145732
  98.7 26.8 %all-to-all-start = ((f32[32,32,256]{2,0,1:T(8,128)}), f32[32,32,256]{2,0,1:T(8,128)S(1)}, u32[]{:S(2)}, u32[]{:S(2)}) async-start(f32[32,32,256]{2,0,1:T(8,128)} %copy.94), calls=%async_computation | async-start | bytes 2097152 | tf_op jit(solution)/shard_map/all_to_all | solution.py:67
  228.4 7.6 copy-start.10
  228.4 7.8 copy-start.11
  232.0 21.3 %all-to-all-start.1 = ((f32[32,32,256]{2,0,1:T(8,128)}), f32[32,32,256]{2,0,1:T(8,128)S(1)}, u32[]{:S(2)}, u32[]{:S(2)}) async-start(f32[32,32,256]{2,0,1:T(8,128)} %copy.100), calls=%async_computation.1 | async-start | bytes 2097152 | tf_op jit(solution)/shard_map/all_to_all | solution.py:74
  236.2 40.3 %copy-start.5 = (s32[96]{0:T(128)}, s32[96]{0:T(128)S(1)}, u32[]{:S(2)}) copy-start(s32[96]{0:T(128)S(1)} %reshape.773) | copy-start | bytes 1156
  289.5 139.7 %all-to-all-start.2 = ((f32[32,32,256]{2,0,1:T(8,128)}), f32[32,32,256]{2,0,1:T(8,128)}, u32[]{:S(2)}, u32[]{:S(2)}) async-start(f32[32,32,256]{2,0,1:T(8,128)} %copy.104), calls=%async_computation.2 | async-start | bytes 2097152 | tf_op jit(solution)/shard_map/all_to_all | solution.py:92
  544.1 116.6 %all-to-all-start.3 = ((f32[32,32,256]{2,0,1:T(8,128)}), f32[32,32,256]{2,0,1:T(8,128)}, u32[]{:S(2)}, u32[]{:S(2)}) async-start(f32[32,32,256]{2,0,1:T(8,128)} %copy.110), calls=%async_computation.3 | async-start | bytes 2097152 | tf_op jit(solution)/shard_map/all_to_all | solution.py:126
  554.0 29.9 %copy-start.1 = (f32[16,6,512]{2,0,1:T(8,128)S(1)}, f32[16,6,512]{2,0,1:T(8,128)}, u32[]{:S(2)}) copy-start(f32[16,6,512]{2,0,1:T(8,128)} %param.11) | copy-start | bytes 589828
  618.4 5.1 copy-start.6
  778.0 200.0 %copy-start.3 = (f32[32]{0:T(128)}, f32[32]{0:T(128)S(1)}, u32[]{:S(2)}) copy-start(f32[32]{0:T(128)S(1)} %div.39) | copy-start | bytes 388
  1055.2 8.7 copy-start.12
  1055.2 59.2 %copy-start.8 = (f32[32]{0:T(128)}, f32[32]{0:T(128)S(1)}, u32[]{:S(2)}) copy-start(f32[32]{0:T(128)S(1)} %div.40) | copy-start | bytes 388
  1206.3 111.1 %all-to-all-start.7 = ((f32[32,32,256]{2,0,1:T(8,128)}), f32[32,32,256]{2,0,1:T(8,128)}, u32[]{:S(2)}, u32[]{:S(2)}) async-start(f32[32,32,256]{2,0,1:T(8,128)} %copy.139), calls=%async_computation.7 | async-start | bytes 2097152 | tf_op jit(solution)/shard_map/all_to_all | solution.py:126
  1240.8 34.3 %copy-start.2 = (s32[3072]{0:T(1024)S(1)}, s32[3072]{0:T(1024)}, u32[]{:S(2)}) copy-start(s32[3072]{0:T(1024)} %all-reduce) | copy-start | bytes 36868
  1244.9 35.3 %copy-start.7 = (s32[96]{0:T(128)S(1)}, s32[96]{0:T(128)}, u32[]{:S(2)}) copy-start(s32[96]{0:T(128)} %copy-done.5) | copy-start | bytes 1156
  1321.0 20.5 %copy-start.9 = (f32[32]{0:T(128)S(1)}, f32[32]{0:T(128)}, u32[]{:S(2)}) copy-start(f32[32]{0:T(128)} %copy-done.8) | copy-start | bytes 388
  1341.5 78.5 %copy-start.13 = (f32[32]{0:T(128)S(1)}, f32[32]{0:T(128)}, u32[]{:S(2)}) copy-start(f32[32]{0:T(128)} %copy-done.12) | copy-start | bytes 388
  1341.5 78.5 %copy-start.4 = (f32[32]{0:T(128)S(1)}, f32[32]{0:T(128)}, u32[]{:S(2)}) copy-start(f32[32]{0:T(128)} %copy-done.3) | copy-start | bytes 388
where the time goes:
time: 1520 us; the launch traced here: 1500 us
  local copies, waits for them, and re-layouts  749 us (49%)
  blocking collectives  438 us (29%)
  other arithmetic  179 us (12%)
  matrix products  68.4 us (5%)
  starting transfers between devices  32.7 us (2%)
  waiting for transfers between devices  32.7 us (2%)
    gather x8, local copies, waits for them, and re-layouts, to_rows(): return vector[:, slot_of_row]  238 us
    gather x7, local copies, waits for them, and re-layouts, to_slots(): return vector[:, row_of_slot]  209 us
    rev x8, local copies, waits for them, and re-layouts, finish_pairs(): received.reshape(load_count, dev_rows // 2, 2)[:, :, ::-1]  164 us
    psum x2, blocking collectives, energy_of(): return lax.psum(jnp.sum(residual * precond, axis=1), ('set', 'sub'))  128 us
    unnamed x1, blocking collectives  127 us
    psum x1, blocking collectives, body(): curvature = lax.psum(jnp.sum(direction * image, axis=1), ('set', 'sub'))  63.8 us
    all_gather x2, blocking collectives, body(): gathered = lax.all_gather(local_coarse_part, 'sub', axis=1, tiled=True)  51.2 us
    dot_general x4, matrix products, apply_factor(): jnp.einsum('gzf,zbf->gzb', half_product, cholesky_factor, preferred_eleme...  44.2 us
  transfers between devices with their start and end apart: 5, of which 2 were waited for; matrix products, arithmetic and copies ran while one was open for 11% of the time, Pallas kernels for 0%

commit v1 on v0

v1 whole, which is shorter than its diff:
```python
import jax
import jax.numpy as jnp
from jax import lax
from jax.experimental import pallas as pl
from jax.experimental.pallas import tpu as pltpu
from jax.sharding import PartitionSpec as P

f32 = jnp.float32
bf16 = jnp.bfloat16
MESH = pl.DeviceIdType.MESH
HI = lax.Precision.HIGHEST

L = 32
PEERS = 32
SETS = 4
CAP = 256
RD = 8192
SD = 16
RM = 512
NC = 8
NK = SD * NC
NCO = 512
GROUP = 8
GROUPS = PEERS // GROUP

NT = (((1,), (1,)), ((), ()))


def dot(a, b):
    return jnp.dot(a, b, preferred_element_type=f32)


def dot_nt(a, b):
    return lax.dot_general(a, b, NT, preferred_element_type=f32)


def at(i, n):
    return pl.ds(pl.multiple_of(i * n, n), n)


def loop(n, f):
    def step(i, carry):
        f(i)
        return carry

    lax.fori_loop(0, n, step, 0)


def split(x):
    high = x.astype(bf16)
    return high, (x - high.astype(f32)).astype(bf16)


def kernel(
    jump, w_hbm, s_hbm, blocks, factor, slot, counts, corner,
    mult, resid,
    W, V, B, BT, Xm, live, jr, f, p, d, kd, pk,
    send, recv, csend, crecv, cpad, crow, Cbd, Ce, OHT,
    gsend, grecv, gall, back, pks, psend, precv, qsend, qrecv, acc,
    wsem, ssem, rsem, qssem, qrsem,
):
    st = lax.axis_index("set")
    me = lax.axis_index("sub")
    mg = me // GROUP

    copy_v = pltpu.make_async_copy(s_hbm, V, wsem.at[0])
    copy_w = pltpu.make_async_copy(w_hbm, W, wsem.at[1])
    copy_v.start()
    copy_w.start()

    barrier = pltpu.get_barrier_semaphore()

    def greet(k):
        pl.semaphore_signal(
            barrier, inc=1, device_id=(st, lax.rem(me + 1 + k, PEERS)), device_id_type=MESH
        )

    def greet_set(k):
        pl.semaphore_signal(
            barrier, inc=1, device_id=(lax.rem(st + 1 + k, SETS), me), device_id_type=MESH
        )

    loop(PEERS - 1, greet)
    loop(SETS - 1, greet_set)

    def remote(e, src, dst, q):
        return pltpu.make_async_remote_copy(
            src_ref=src, dst_ref=dst, send_sem=ssem.at[e, q], recv_sem=rsem.at[e, me],
            device_id=(st, q), device_id_type=MESH,
        )

    def arrival(e, dst, q):
        return pltpu.make_async_remote_copy(
            src_ref=dst, dst_ref=dst, send_sem=ssem.at[e, q], recv_sem=rsem.at[e, q],
            device_id=(st, q), device_id_type=MESH,
        )

    def others(f):
        def one(k):
            f(lax.rem(me + 1 + k, PEERS))

        loop(PEERS - 1, one)

    def group_others(g, f):
        def one(k):
            q = g * GROUP + lax.rem(me + k, GROUP)

            @pl.when(q != me)
            def _():
                f(q)

        loop(GROUP, one)

    def swap_pairs(x):
        lane = lax.broadcasted_iota(jnp.int32, x.shape, 1)
        n = x.shape[1]
        return jnp.where(lane % 2 == 0, pltpu.roll(x, n - 1, 1), pltpu.roll(x, 1, 1))

    def slots_and_send(e, x):
        def one(i):
            g = lax.rem(mg + i, GROUPS)
            for c in range(RD // CAP):
                cols = slice(c * CAP, (c + 1) * CAP)
                a = jnp.broadcast_to(slot[0:1, cols] // CAP - g * GROUP, (L, CAP))
                v = x[:, cols]
                Xm[:, cols] = jnp.concatenate(
                    [jnp.where(a == k, v, 0.0).astype(bf16) for k in range(GROUP)], axis=0
                )
            send[pl.ds(g * GROUP, GROUP)] = dot(Xm[...], BT[...]).reshape(GROUP, L, CAP)
            group_others(g, lambda q: remote(e, send.at[q], recv.at[e % 2, me], q).start())

        loop(GROUPS, one)
        recv[e % 2, me] = swap_pairs(send[me])

    def sent(e):
        others(lambda q: remote(e, send.at[q], recv.at[e % 2, me], q).wait_send())

    def rows_of_group(g, blocks16, out, first):
        for c in range(RD // CAP):
            cols = slice(c * CAP, (c + 1) * CAP)
            a = jnp.broadcast_to(slot[0:1, cols] // CAP - g * GROUP, (L, CAP))
            u = dot(blocks16, B[:, cols])
            res = out[:, cols]
            for k in range(GROUP):
                res = jnp.where(a == k, u[k * L : (k + 1) * L], res)
            out[:, cols] = res

    def receive_rows(e, out):
        out[...] = jnp.zeros_like(out)

        def one(i):
            g = lax.rem(mg + GROUPS - i, GROUPS)
            group_others(g, lambda q: arrival(e, recv.at[e % 2, q], q).wait_recv())
            blk = recv[e % 2, pl.ds(g * GROUP, GROUP)].reshape(GROUP * L, CAP).astype(bf16)
            rows_of_group(g, blk, out, False)

        loop(GROUPS, one)
        sent(e)

    def apply(x, F, scale):
        acc[...] = jnp.zeros_like(acc)

        def one(i):
            for k in range(4):
                s = i * 4 + k
                cols = at(s, RM)
                v = x[:, cols] * scale
                m = F[s]
                t = dot(v.astype(bf16), m).astype(bf16)
                out = dot_nt(t, m)
                f[:, cols] = out
                prod = v * out
                acc[...] += sum(prod[:, n * 128 : (n + 1) * 128] for n in range(RM // 128))

        loop(SD // 4, one)

    def lanes_to_row(x):
        x = jnp.concatenate([x, jnp.zeros((128 - L, 128), f32)], axis=0)
        return jnp.broadcast_to(jnp.sum(x.T, axis=0, keepdims=True), (8, 128))

    def row_to_column(x):
        return jnp.broadcast_to(x[0:1], (128, 128)).T[0:L]

    def sum_start(e):
        psend[e] = lanes_to_row(acc[...])
        precv[e, me] = psend[e]
        others(lambda q: remote(8 + e, psend.at[e], precv.at[e, me], q).start())

    def across(e, q):
        return pltpu.make_async_remote_copy(
            src_ref=qsend.at[e], dst_ref=qrecv.at[e, st], send_sem=qssem.at[e, q],
            recv_sem=qrsem.at[e, st], device_id=(q, me), device_id_type=MESH,
        )

    def across_arrival(e, q):
        return pltpu.make_async_remote_copy(
            src_ref=qsend.at[e], dst_ref=qrecv.at[e, q], send_sem=qssem.at[e, q],
            recv_sem=qrsem.at[e, q], device_id=(q, me), device_id_type=MESH,
        )

    def other_sets(f):
        loop(SETS - 1, lambda k: f(lax.rem(st + 1 + k, SETS)))

    def sum_middle(e, extra):
        others(lambda q: arrival(8 + e, precv.at[e, q], q).wait_recv())
        others(lambda q: remote(8 + e, psend.at[e], precv.at[e, me], q).wait_send())
        total = jnp.sum(precv[e], axis=0)
        if extra is not None:
            total = total + extra
        qsend[e] = total
        qrecv[e, st] = total
        other_sets(lambda q: across(e, q).start())

    def sum_end(e):
        other_sets(lambda q: across_arrival(e, q).wait_recv())
        other_sets(lambda q: across(e, q).wait_send())
        return row_to_column(jnp.sum(qrecv[e], axis=0))

    def coarse_start(e):
        gsend[e] = dot_nt(d[...].astype(bf16), Cbd[...])
        grecv[e, me] = gsend[e]
        others(lambda q: remote(6 + e, gsend.at[e], grecv.at[e, me], q).start())

    def coarse_solve(e):
        others(lambda q: arrival(6 + e, grecv.at[e, q], q).wait_recv())
        others(lambda q: remote(6 + e, gsend.at[e], grecv.at[e, me], q).wait_send())
        for j in range(PEERS):
            high, low = split(grecv[e, j])
            gall[:, j * NK : (j + 1) * NK] = jnp.concatenate([high, low], axis=0)
        both = dot_nt(gall[...], OHT[...])
        middle = jnp.dot(both[:L] + both[L:], factor[...], precision=HI, preferred_element_type=f32)
        sol = lax.dot_general(
            middle, factor[...], NT, precision=HI, preferred_element_type=f32
        )
        both = dot(jnp.concatenate(split(sol), axis=0), OHT[...])
        back[...] = both[:L] + both[L:]
        kd[...] = dot(back[:, at(me, NK)].astype(bf16), Cbd[...])
        square = middle * middle
        return lanes_to_row(sum(square[:, n * 128 : (n + 1) * 128] for n in range(NCO // 128)))

    def partners_coarse():
        def one(j):
            pks[pl.ds(pl.multiple_of(j * L, L), L), :] = dot(
                back[:, at(j, NK)].astype(bf16), Ce[j]
            ).astype(bf16)

        loop(PEERS, one)
        pk[...] = jnp.zeros_like(pk)
        loop(
            GROUPS,
            lambda g: rows_of_group(g, pks[at(g, GROUP * L), :], pk, False),
        )

    def onehot(c):
        cols = at(c, CAP)
        hit = lax.broadcasted_iota(jnp.int32, (CAP, CAP), 0) == slot[0:1, cols] % CAP
        m = jnp.where(hit, 1.0, 0.0)
        B[:, cols] = m.astype(bf16)
        BT[cols, :] = m.T.astype(bf16)

    loop(RD // CAP, onehot)

    def live_rows(c):
        cols = at(c, RM)
        s = slot[0:1, cols]
        a = s // CAP
        n = jnp.zeros_like(s)
        for k in range(PEERS):
            n = jnp.where(a == k, counts[0, k], n)
        on = jnp.where(s % CAP < n, 1.0, 0.0)
        live[:, cols] = jnp.broadcast_to(on, (8, RM))
        resid[:, cols] = on * jump[:, cols]

    loop(RD // RM, live_rows)

    cpad[...] = jnp.zeros_like(cpad)
    for s in range(SD):
        cpad[s, 0:6, :] = blocks[s]
    Cbd[...] = jnp.zeros_like(Cbd)
    zero = jnp.zeros((NC, RM), f32)
    row = lax.broadcasted_iota(jnp.int32, (NC, RM), 0)
    for s in range(SD):
        crow[:, s * RM : (s + 1) * RM] = jnp.where(row == 6, float(s), cpad[s])
    for q in range(SD // 2):
        top = jnp.concatenate([cpad[2 * q], zero], axis=1)
        low = jnp.concatenate([zero, cpad[2 * q + 1]], axis=1)
        Cbd[2 * q * NC : (2 * q + 2) * NC, 2 * q * RM : (2 * q + 2) * RM] = jnp.concatenate(
            [top, low], axis=0
        ).astype(bf16)

    pl.semaphore_wait(barrier, PEERS - 1 + SETS - 1)

    slots_and_send(0, resid)

    def mask_modes(c):
        cols = at(c, CAP)
        a = jnp.broadcast_to(slot[0:1, cols] // CAP, (NC, CAP))
        v = crow[:, cols]
        Xm[:, cols] = jnp.concatenate(
            [jnp.where(a == k, v, 0.0) for k in range(PEERS)], axis=0
        ).astype(bf16)

    loop(RD // CAP, mask_modes)
    csend[...] = dot(Xm[...], BT[...]).reshape(PEERS, NC, CAP)
    csend[:, 7:8, 0:NK] = jnp.broadcast_to(corner[0:1].reshape(1, 1, NK), (PEERS, 1, NK))
    others(lambda q: remote(5, csend.at[q], crecv.at[me], q).start())
    crecv[me] = swap_pairs(csend[me])
    crecv[me, 7:8, 0:NK] = corner[0:1]

    receive_rows(0, p)

    def first(c):
        cols = at(c, RM)
        jr[:, cols] = resid[:, cols] + live[0:1, cols] * p[:, cols]

    loop(RD // RM, first)

    copy_v.wait()
    apply(jr, V, 1.0)
    sum_start(0)
    slots_and_send(1, f)

    others(lambda q: arrival(5, crecv.at[q], q).wait_recv())
    others(lambda q: remote(5, csend.at[q], crecv.at[me], q).wait_send())

    def expand(j):
        blk = crecv[j]
        sub = jnp.broadcast_to(blk[6:7], (NC, CAP))
        for q in range(SD // 2):
            Ce[j, 2 * q * NC : (2 * q + 2) * NC, :] = jnp.concatenate(
                [jnp.where(sub == float(2 * q), blk, 0.0),
                 jnp.where(sub == float(2 * q + 1), blk, 0.0)], axis=0
            ).astype(bf16)
        unknown = lax.broadcasted_iota(jnp.int32, (NCO, NK), 0).astype(f32)
        OHT[:, at(j, NK)] = jnp.where(unknown == blk[7:8, 0:NK], 1.0, 0.0).astype(bf16)

    loop(PEERS, expand)

    receive_rows(1, p)

    def first_direction(c):
        cols = at(c, RM)
        d[:, cols] = live[0:1, cols] * (f[:, cols] + p[:, cols])

    loop(RD // RM, first_direction)

    copy_w.wait()
    coarse_start(0)
    apply(d, W, 2.0)
    sum_start(1)
    slots_and_send(2, f)
    square = coarse_solve(0)
    sum_middle(0, None)
    sum_middle(1, square)
    partners_coarse()
    energy = sum_end(0)
    alpha = energy / sum_end(1)
    receive_rows(2, p)

    def update(c):
        cols = at(c, RM)
        on = live[0:1, cols]
        al = alpha[:, 0:1]
        jf = f[:, cols] + p[:, cols]
        k = kd[:, cols]
        mult[:, cols] = al * d[:, cols]
        resid[:, cols] -= al * (on * (jf + k))
        jr[:, cols] -= al * (on * (2.0 * jf + k + pk[:, cols]))

    loop(RD // RM, update)

    apply(jr, V, 1.0)
    sum_start(2)
    slots_and_send(3, f)
    sum_middle(2, None)
    new = sum_end(2)
    receive_rows(3, p)
    beta = new / energy

    def next_direction(c):
        cols = at(c, RM)
        d[:, cols] = live[0:1, cols] * (f[:, cols] + p[:, cols]) + beta[:, 0:1] * d[:, cols]

    loop(RD // RM, next_direction)

    coarse_start(1)
    apply(d, W, 2.0)
    sum_start(3)
    slots_and_send(4, f)
    square = coarse_solve(1)
    sum_middle(3, square)
    alpha2 = new / sum_end(3)
    receive_rows(4, p)

    def last(c):
        cols = at(c, RM)
        al = alpha2[:, 0:1]
        mult[:, cols] += al * d[:, cols]
        resid[:, cols] -= al * (live[0:1, cols] * (f[:, cols] + p[:, cols] + kd[:, cols]))

    loop(RD // RM, last)


def body(
    jump_rhs, w_factor, s_factor, rigid_coarse_blocks, coarse_factor, slot_of_row, pair_counts,
    corner_map,
):
    slot = slot_of_row.reshape(1, RD)
    corner = jnp.pad(corner_map.astype(f32), ((0, 0), (0, 2)), constant_values=-1.0)
    corner = jnp.broadcast_to(corner.reshape(1, NK), (8, NK))
    vm = pl.BlockSpec(memory_space=pltpu.VMEM)
    hbm = pl.BlockSpec(memory_space=pl.ANY)
    sm = pl.BlockSpec(memory_space=pltpu.SMEM)
    V = pltpu.VMEM
    vec = V((L, RD), f32)
    return pl.pallas_call(
        kernel,
        out_shape=(jax.ShapeDtypeStruct((L, RD), f32),) * 2,
        in_specs=[vm, hbm, hbm, vm, vm, vm, sm, vm],
        out_specs=[vm, vm],
        scratch_shapes=[
            V((SD, RM, RM), bf16), V((SD, RM, RM), bf16), V((CAP, RD), bf16), V((RD, CAP), bf16),
            V((GROUP * L, RD), bf16), V((8, RD), f32), vec, vec, vec, vec, vec, vec,
            V((PEERS, L, CAP), f32), V((2, PEERS, L, CAP), f32), V((PEERS, NC, CAP), f32),
            V((PEERS, NC, CAP), f32), V((SD, NC, RM), f32), V((NC, RD), f32), V((NK, RD), bf16),
            V((PEERS, NK, CAP), bf16), V((NCO, PEERS * NK), bf16),
            V((2, L, NK), f32), V((2, PEERS, L, NK), f32), V((2 * L, PEERS * NK), bf16),
            V((L, PEERS * NK), f32), V((PEERS * L, CAP), bf16),
            V((4, 8, 128), f32), V((4, PEERS, 8, 128), f32), V((4, 8, 128), f32),
            V((4, SETS, 8, 128), f32), V((L, 128), f32),
            pltpu.SemaphoreType.DMA((2,)), pltpu.SemaphoreType.DMA((12, PEERS)),
            pltpu.SemaphoreType.DMA((12, PEERS)), pltpu.SemaphoreType.DMA((4, SETS)),
            pltpu.SemaphoreType.DMA((4, SETS)),
        ],
        compiler_params=pltpu.CompilerParams(
            collective_id=0, has_side_effects=True, vmem_limit_bytes=62 << 20
        ),
        cost_estimate=pl.CostEstimate(
            flops=60_000_000_000, bytes_accessed=20 << 20, transcendentals=0
        ),
    )(jump_rhs, w_factor, s_factor, rigid_coarse_blocks, coarse_factor, slot, pair_counts, corner)


def solution(mesh):
    each = ("set", "sub")
    return jax.shard_map(
        body,
        mesh=mesh,
        in_specs=(
            P(None, each), P(each, None, None), P(each, None, None), P(each, None, None),
            P("set", None), P(each), P(each, None), P(each, None),
        ),
        out_specs=(P(None, each), P(None, each)),
        check_vma=False,
    )
```

time: 1520 us -> 167 us (0.11); the launches traced: 1500 us -> 167 us
  local copies, waits for them, and re-layouts: 749 us -> 7.05 us
  blocking collectives: 438 us -> 0 us
  other arithmetic: 179 us -> 0.69 us
  Pallas kernels: 0 us -> 159 us
  matrix products: 68.4 us -> 0 us
  starting transfers between devices: 32.7 us -> 0 us
  waiting for transfers between devices: 32.7 us -> 0 us
    gather x19 -> x0, local copies, waits for them, and re-layouts: 455 us -> none  [the longest x8 238 us: to_rows(): return vector[:, slot_of_row]]
    psum x3 -> x0, blocking collectives: 192 us -> none  [the longest x2 128 us: energy_of(): return lax.psum(jnp.sum(residual * precond, axis=1), ('set', 'sub'))]
    rev x8 -> x0, local copies, waits for them, and re-layouts: 164 us -> none  [finish_pairs(): received.reshape(load_count, dev_rows // 2, 2)[:, :, ::-1]]
    pallas_call x0 -> x1, Pallas kernels: none -> 159 us  [body(): pl.pallas_call(kernel, out_shape=(jax.ShapeDtypeStruct((L, RD), f32),) *...]
    unnamed x1 -> x0, blocking collectives: 127 us -> none
    dot_general x16 -> x0, matrix products: 68.4 us -> none  [the longest x4 44.2 us: apply_factor(): jnp.einsum('gzf,zbf->gzb', half_product, cholesky_factor, preferred_eleme...]
    all_to_all x3 -> x0, blocking collectives: 67.5 us -> none  [the longest x1 22.8 us: precondition(): lax.all_to_all(shaped, 'sub', split_axis=1, concat_axis=1, tiled=True)]
    mul x6 -> x0, other arithmetic: 61.8 us -> none  [the longest x2 26.1 us: body(): live * (direction + finish_pairs(lax.all_to_all(shaped_dir, 'sub', split_...]
  transfers between devices with their start and end apart: 5 -> 0, of which waited for: 2 -> 0; matrix products, arithmetic and copies ran while one was open for 11% -> 0% of each run, Pallas kernels for 0% -> 0%
where the time goes in v1:
time: 167 us
  Pallas kernels  159 us (95%)
  local copies, waits for them, and re-layouts  7.05 us (4%)
    pallas_call x1, Pallas kernels, body(): pl.pallas_call(kernel, out_shape=(jax.ShapeDtypeStruct((L, RD), f32),) *...  159 us
    unnamed x4, local copies, waits for them, and re-layouts  6.36 us

profile of v1, /device:TPU:1, one launch (start us, length us, event | category | flops | bytes accessed | tf_op | source)
XLA Modules:
  0.0 167.1 jit_solution(15529890798780053729)
XLA Ops:
  0.6 0.7 convert_element_type.3
  1.3 0.1 copy.14
  1.4 0.1 broadcast_in_dim.7
  1.5 0.6 broadcast_in_dim.8.corner
  2.1 1.7 %copy.13.blocks = f32[16,6,512]{2,1,0:T(8,128)} copy(f32[16,6,512]{2,0,1:T(8,128)} %param.11) | data formatting | bytes 393216 | tf_op args[3]
  3.9 158.7 %shard_map.95 = (f32[32,8192]{1,0:T(8,128)}, f32[32,8192]{1,0:T(8,128)}) custom-call(f32[32,8192]{1,0:T(8,128)} %jump.1, bf16[16,512,512]{2,1,0:T(8,128)(2,1)} %w_hbm.1, bf16[16,512,512]{2,1,0:T(8,128)(2,1)} %s_hbm.1, f32[16,6,512]{2,1,0:T(8,128)} %copy.13.blocks, f32[512,512]{1,0:T(8,128)} %factor.1, s32[1,8192]{1,0:T(1,128)} %bitcast.1, s32[1,32]{1,0:T(1,128)} %counts.1, ...), custom_call_target="tpu_custom_call" | custom-call | flops 60000002048 | bytes 20971520 | tf_op jit(solution)/shard_map/pallas_call | solution.py:416
  162.6 2.3 %copy.17 = f32[32,8192]{1,0:T(8,128)} copy(f32[32,8192]{1,0:T(8,128)} %get-tuple-element.4) | data formatting | bytes 2097152
  164.8 2.3 %copy.18 = f32[32,8192]{1,0:T(8,128)} copy(f32[32,8192]{1,0:T(8,128)} %get-tuple-element.5) | data formatting | bytes 2097152
  (1 shorter events, 0.0 us)

commit v2 on v1

--- a/solution.py
+++ b/solution.py
@@ -20,6 +20,7 @@
 NC = 8
 NK = SD * NC
 NCO = 512
+QS = NCO // NK
 GROUP = 8
 GROUPS = PEERS // GROUP
 
@@ -56,7 +57,7 @@
     mult, resid,
     W, V, B, BT, Xm, live, jr, f, p, d, kd, pk,
     send, recv, csend, crecv, cpad, crow, Cbd, Ce, OHT,
-    gsend, grecv, gall, back, pks, psend, precv, qsend, qrecv, acc,
+    gsend, grecv, hsend, hrecv, back, pks, psend, precv, qsend, qrecv, acc,
     wsem, ssem, rsem, qssem, qrsem,
 ):
     st = lax.axis_index("set")
@@ -111,6 +112,9 @@
 
         loop(GROUP, one)
 
+    def plane(i):
+        return jnp.where(i == 0, 2, jnp.where(i == 3, 0, 2 * i - 1))
+
     def swap_pairs(x):
         lane = lax.broadcasted_iota(jnp.int32, x.shape, 1)
         n = x.shape[1]
@@ -118,7 +122,7 @@
 
     def slots_and_send(e, x):
         def one(i):
-            g = lax.rem(mg + i, GROUPS)
+            g = lax.rem(mg + plane(i), GROUPS)
             for c in range(RD // CAP):
                 cols = slice(c * CAP, (c + 1) * CAP)
                 a = jnp.broadcast_to(slot[0:1, cols] // CAP - g * GROUP, (L, CAP))
@@ -149,13 +153,20 @@
         out[...] = jnp.zeros_like(out)
 
         def one(i):
-            g = lax.rem(mg + GROUPS - i, GROUPS)
+            g = lax.rem(mg + GROUPS - plane(i), GROUPS)
             group_others(g, lambda q: arrival(e, recv.at[e % 2, q], q).wait_recv())
             blk = recv[e % 2, pl.ds(g * GROUP, GROUP)].reshape(GROUP * L, CAP).astype(bf16)
             rows_of_group(g, blk, out, False)
 
         loop(GROUPS, one)
         sent(e)
+
+    def gram(F):
+        def one(s):
+            m = F[s]
+            F[s] = dot_nt(m, m).astype(bf16)
+
+        loop(SD, one)
 
     def apply(x, F, scale):
         acc[...] = jnp.zeros_like(acc)
@@ -165,9 +176,7 @@
                 s = i * 4 + k
                 cols = at(s, RM)
                 v = x[:, cols] * scale
-                m = F[s]
-                t = dot(v.astype(bf16), m).astype(bf16)
-                out = dot_nt(t, m)
+                out = dot(v.astype(bf16), F[s])
                 f[:, cols] = out
                 prod = v * out
                 acc[...] += sum(prod[:, n * 128 : (n + 1) * 128] for n in range(RM // 128))
@@ -176,10 +185,10 @@
 
     def lanes_to_row(x):
         x = jnp.concatenate([x, jnp.zeros((128 - L, 128), f32)], axis=0)
-        return jnp.broadcast_to(jnp.sum(x.T, axis=0, keepdims=True), (8, 128))
+        return jnp.sum(x.T, axis=0, keepdims=True)
 
     def row_to_column(x):
-        return jnp.broadcast_to(x[0:1], (128, 128)).T[0:L]
+        return jnp.broadcast_to(x, (128, 128)).T[0:L]
 
     def sum_start(e):
         psend[e] = lanes_to_row(acc[...])
@@ -217,18 +226,40 @@
         return row_to_column(jnp.sum(qrecv[e], axis=0))
 
     def coarse_start(e):
-        gsend[e] = dot_nt(d[...].astype(bf16), Cbd[...])
-        grecv[e, me] = gsend[e]
-        others(lambda q: remote(6 + e, gsend.at[e], grecv.at[e, me], q).start())
+        g = dot_nt(d[...].astype(bf16), Cbd[...])
+        unknown = lax.broadcasted_iota(jnp.int32, (NK, NK), 0)
+        hits = jnp.concatenate(
+            [jnp.where((unknown + q * NK).astype(f32) == corner[0:1], 1.0, 0.0).astype(bf16)
+             for q in range(QS)], axis=1
+        )
+
+        def spread(x):
+            zero = jnp.zeros((L, NK), bf16)
+            return jnp.concatenate(
+                [jnp.concatenate([x if r == q else zero for r in range(QS)], axis=1)
+                 for q in range(QS)], axis=0
+            )
+
+        high, low = split(g)
+        x = dot_nt(hits, spread(high)) + dot_nt(hits, spread(low))
+        for j in range(PEERS):
+            gsend[e, j] = x[j * QS : (j + 1) * QS]
+        grecv[e, me] = gsend[e, me]
+        others(lambda q: remote(6 + e, gsend.at[e, q], grecv.at[e, me], q).start())
+
+    def coarse_sum(e):
+        others(lambda q: arrival(6 + e, grecv.at[e, q], q).wait_recv())
+        hsend[e] = jnp.sum(grecv[e], axis=0)
+        hrecv[e, me] = hsend[e]
+        others(lambda q: remote(12 + e, hsend.at[e], hrecv.at[e, me], q).start())
+        others(lambda q: remote(6 + e, gsend.at[e, q], grecv.at[e, me], q).wait_send())
 
     def coarse_solve(e):
-        others(lambda q: arrival(6 + e, grecv.at[e, q], q).wait_recv())
-        others(lambda q: remote(6 + e, gsend.at[e], grecv.at[e, me], q).wait_send())
-        for j in range(PEERS):
-            high, low = split(grecv[e, j])
-            gall[:, j * NK : (j + 1) * NK] = jnp.concatenate([high, low], axis=0)
-        both = dot_nt(gall[...], OHT[...])
-        middle = jnp.dot(both[:L] + both[L:], factor[...], precision=HI, preferred_element_type=f32)
+        others(lambda q: arrival(12 + e, hrecv.at[e, q], q).wait_recv())
+        others(lambda q: remote(12 + e, hsend.at[e], hrecv.at[e, me], q).wait_send())
+        x = jnp.concatenate([hrecv[e, j] for j in range(PEERS)], axis=0).T
+        coarse_in = jnp.concatenate([x[q * L : (q + 1) * L] for q in range(QS)], axis=1)
+        middle = jnp.dot(coarse_in, factor[...], precision=HI, preferred_element_type=f32)
         sol = lax.dot_general(
             middle, factor[...], NT, precision=HI, preferred_element_type=f32
         )
@@ -275,7 +306,8 @@
 
     cpad[...] = jnp.zeros_like(cpad)
     for s in range(SD):
-        cpad[s, 0:6, :] = blocks[s]
+        for k in range(6):
+            cpad[s, k : k + 1, :] = blocks[k, s : s + 1, :]
     Cbd[...] = jnp.zeros_like(Cbd)
     zero = jnp.zeros((NC, RM), f32)
     row = lax.broadcasted_iota(jnp.int32, (NC, RM), 0)
@@ -303,11 +335,13 @@
     loop(RD // CAP, mask_modes)
     csend[...] = dot(Xm[...], BT[...]).reshape(PEERS, NC, CAP)
     csend[:, 7:8, 0:NK] = jnp.broadcast_to(corner[0:1].reshape(1, 1, NK), (PEERS, 1, NK))
-    others(lambda q: remote(5, csend.at[q], crecv.at[me], q).start())
     crecv[me] = swap_pairs(csend[me])
     crecv[me, 7:8, 0:NK] = corner[0:1]
 
+    copy_v.wait()
+    gram(V)
     receive_rows(0, p)
+    others(lambda q: remote(5, csend.at[q], crecv.at[me], q).start())
 
     def first(c):
         cols = at(c, RM)
@@ -315,7 +349,6 @@
 
     loop(RD // RM, first)
 
-    copy_v.wait()
     apply(jr, V, 1.0)
     sum_start(0)
     slots_and_send(1, f)
@@ -335,6 +368,8 @@
         OHT[:, at(j, NK)] = jnp.where(unknown == blk[7:8, 0:NK], 1.0, 0.0).astype(bf16)
 
     loop(PEERS, expand)
+    copy_w.wait()
+    gram(W)
 
     receive_rows(1, p)
 
@@ -344,11 +379,11 @@
 
     loop(RD // RM, first_direction)
 
-    copy_w.wait()
     coarse_start(0)
     apply(d, W, 2.0)
     sum_start(1)
     slots_and_send(2, f)
+    coarse_sum(0)
     square = coarse_solve(0)
     sum_middle(0, None)
     sum_middle(1, square)
@@ -387,6 +422,7 @@
     apply(d, W, 2.0)
     sum_start(3)
     slots_and_send(4, f)
+    coarse_sum(1)
     square = coarse_solve(1)
     sum_middle(3, square)
     alpha2 = new / sum_end(3)
@@ -407,7 +443,8 @@
 ):
     slot = slot_of_row.reshape(1, RD)
     corner = jnp.pad(corner_map.astype(f32), ((0, 0), (0, 2)), constant_values=-1.0)
-    corner = jnp.broadcast_to(corner.reshape(1, NK), (8, NK))
+    corner = corner.reshape(1, NK)
+    rigid_coarse_blocks = jnp.transpose(rigid_coarse_blocks, (1, 0, 2))
     vm = pl.BlockSpec(memory_space=pltpu.VMEM)
     hbm = pl.BlockSpec(memory_space=pl.ANY)
     sm = pl.BlockSpec(memory_space=pltpu.SMEM)
@@ -424,12 +461,13 @@
             V((PEERS, L, CAP), f32), V((2, PEERS, L, CAP), f32), V((PEERS, NC, CAP), f32),
             V((PEERS, NC, CAP), f32), V((SD, NC, RM), f32), V((NC, RD), f32), V((NK, RD), bf16),
             V((PEERS, NK, CAP), bf16), V((NCO, PEERS * NK), bf16),
-            V((2, L, NK), f32), V((2, PEERS, L, NK), f32), V((2 * L, PEERS * NK), bf16),
+            V((2, PEERS, QS, NK), f32), V((2, PEERS, QS, NK), f32), V((2, QS, NK), f32),
+            V((2, PEERS, QS, NK), f32),
             V((L, PEERS * NK), f32), V((PEERS * L, CAP), bf16),
-            V((4, 8, 128), f32), V((4, PEERS, 8, 128), f32), V((4, 8, 128), f32),
-            V((4, SETS, 8, 128), f32), V((L, 128), f32),
-            pltpu.SemaphoreType.DMA((2,)), pltpu.SemaphoreType.DMA((12, PEERS)),
-            pltpu.SemaphoreType.DMA((12, PEERS)), pltpu.SemaphoreType.DMA((4, SETS)),
+            V((4, 1, 128), f32), V((4, PEERS, 1, 128), f32), V((4, 1, 128), f32),
+            V((4, SETS, 1, 128), f32), V((L, 128), f32),
+            pltpu.SemaphoreType.DMA((2,)), pltpu.SemaphoreType.DMA((14, PEERS)),
+            pltpu.SemaphoreType.DMA((14, PEERS)), pltpu.SemaphoreType.DMA((4, SETS)),
             pltpu.SemaphoreType.DMA((4, SETS)),
         ],
         compiler_params=pltpu.CompilerParams(

time: 167 us -> 177 us (1.060)
  Pallas kernels: 159 us -> 170 us
  local copies, waits for them, and re-layouts: 7.05 us -> 5.22 us
    pallas_call x1, Pallas kernels: 159 us -> 170 us  [body(): pl.pallas_call(kernel, out_shape=(jax.ShapeDtypeStruct((L, RD), f32),) *...]
    unnamed x4 -> x3, local copies, waits for them, and re-layouts: 6.36 us -> 4.61 us
where the time goes in v2:
time: 177 us
  Pallas kernels  170 us (96%)
  local copies, waits for them, and re-layouts  5.22 us (3%)
    pallas_call x1, Pallas kernels, body(): pl.pallas_call(kernel, out_shape=(jax.ShapeDtypeStruct((L, RD), f32),) *...  170 us
    unnamed x3, local copies, waits for them, and re-layouts  4.61 us

profile of v2, /device:TPU:1, one launch (start us, length us, event | category | flops | bytes accessed | tf_op | source)
XLA Modules:
  0.0 176.6 jit_solution(15940777784099526299)
XLA Ops:
  0.6 0.7 convert_element_type.3
  1.3 0.1 copy.12
  1.4 0.6 reshape.11.corner
  2.0 170.1 %shard_map.95 = (f32[32,8192]{1,0:T(8,128)}, f32[32,8192]{1,0:T(8,128)}) custom-call(f32[32,8192]{1,0:T(8,128)} %jump.1, bf16[16,512,512]{2,1,0:T(8,128)(2,1)} %w_hbm.1, bf16[16,512,512]{2,1,0:T(8,128)(2,1)} %s_hbm.1, f32[6,16,512]{2,1,0:T(8,128)} %bitcast.2, f32[512,512]{1,0:T(8,128)} %factor.1, s32[1,8192]{1,0:T(1,128)} %bitcast.3, s32[1,32]{1,0:T(1,128)} %counts.1, ...), custom_call_target="tpu_custom_call" | custom-call | flops 60000002048 | bytes 20971520 | tf_op jit(solution)/shard_map/pallas_call | solution.py:453
  172.1 2.3 %copy.15 = f32[32,8192]{1,0:T(8,128)} copy(f32[32,8192]{1,0:T(8,128)} %get-tuple-element.4) | data formatting | bytes 2097152
  174.4 2.3 %copy.16 = f32[32,8192]{1,0:T(8,128)} copy(f32[32,8192]{1,0:T(8,128)} %get-tuple-element.5) | data formatting | bytes 2097152
  (1 shorter events, 0.0 us)

commit v3 on v2

--- a/solution.py
+++ b/solution.py
@@ -57,8 +57,8 @@
     mult, resid,
     W, V, B, BT, Xm, live, jr, f, p, d, kd, pk,
     send, recv, csend, crecv, cpad, crow, Cbd, Ce, OHT,
-    gsend, grecv, hsend, hrecv, back, pks, psend, precv, qsend, qrecv, acc,
-    wsem, ssem, rsem, qssem, qrsem,
+    gsend, grecv, hsend, hrecv, back, pks, psend, precv, qsend, qrecv, acc, acc0,
+    sa, wsem, assem, arsem, ssem, rsem, qssem, qrsem,
 ):
     st = lax.axis_index("set")
     me = lax.axis_index("sub")
@@ -84,33 +84,47 @@
     loop(PEERS - 1, greet)
     loop(SETS - 1, greet_set)
 
-    def remote(e, src, dst, q):
+    def wrap(q):
+        return jnp.where(q >= PEERS, q - PEERS, q)
+
+    def others(f):
+        for k in range(1, PEERS):
+            f(wrap(me + k))
+
+    def send_all(n, src, dst):
+        others(
+            lambda q: pltpu.make_async_remote_copy(
+                src_ref=src(q), dst_ref=dst, send_sem=ssem.at[n], recv_sem=rsem.at[n],
+                device_id=(st, q), device_id_type=MESH,
+            ).start()
+        )
+
+    def wait_all(n, dst):
+        copy = pltpu.make_async_remote_copy(
+            src_ref=dst, dst_ref=dst, send_sem=ssem.at[n], recv_sem=rsem.at[n],
+            device_id=(st, wrap(me + 1)), device_id_type=MESH,
+        )
+        copy.wait_recv()
+        copy.wait_send()
+
+    def block_copy(e, src, dst, g, q):
         return pltpu.make_async_remote_copy(
-            src_ref=src, dst_ref=dst, send_sem=ssem.at[e, q], recv_sem=rsem.at[e, me],
+            src_ref=src, dst_ref=dst, send_sem=assem.at[e], recv_sem=arsem.at[e, g],
             device_id=(st, q), device_id_type=MESH,
         )
 
-    def arrival(e, dst, q):
-        return pltpu.make_async_remote_copy(
-            src_ref=dst, dst_ref=dst, send_sem=ssem.at[e, q], recv_sem=rsem.at[e, q],
-            device_id=(st, q), device_id_type=MESH,
-        )
-
-    def others(f):
-        def one(k):
-            f(lax.rem(me + 1 + k, PEERS))
-
-        loop(PEERS - 1, one)
-
-    def group_others(g, f):
-        def one(k):
-            q = g * GROUP + lax.rem(me + k, GROUP)
+    def send_group(e, g):
+        for k in range(GROUP):
+            r = lax.rem(me, GROUP) + k
+            q = g * GROUP + jnp.where(r >= GROUP, r - GROUP, r)
 
             @pl.when(q != me)
             def _():
-                f(q)
-
-        loop(GROUP, one)
+                block_copy(e, send.at[q], recv.at[e % 2, me], mg, q).start()
+
+    def wait_group(e, g, n):
+        some = recv.at[e % 2, pl.ds(g * GROUP, n)]
+        block_copy(e, some, some, g, wrap(me + 1)).wait_recv()
 
     def plane(i):
         return jnp.where(i == 0, 2, jnp.where(i == 3, 0, 2 * i - 1))
@@ -120,29 +134,32 @@
         n = x.shape[1]
         return jnp.where(lane % 2 == 0, pltpu.roll(x, n - 1, 1), pltpu.roll(x, 1, 1))
 
-    def slots_and_send(e, x):
+    def slots_and_send(e, x, early=None):
         def one(i):
             g = lax.rem(mg + plane(i), GROUPS)
             for c in range(RD // CAP):
                 cols = slice(c * CAP, (c + 1) * CAP)
-                a = jnp.broadcast_to(slot[0:1, cols] // CAP - g * GROUP, (L, CAP))
+                a = jnp.concatenate([sa[:, cols] - g * GROUP] * (L // 8), axis=0)
                 v = x[:, cols]
                 Xm[:, cols] = jnp.concatenate(
                     [jnp.where(a == k, v, 0.0).astype(bf16) for k in range(GROUP)], axis=0
                 )
             send[pl.ds(g * GROUP, GROUP)] = dot(Xm[...], BT[...]).reshape(GROUP, L, CAP)
-            group_others(g, lambda q: remote(e, send.at[q], recv.at[e % 2, me], q).start())
+            if early is not None:
+                pl.when(i == 0)(early)
+            send_group(e, g)
 
         loop(GROUPS, one)
         recv[e % 2, me] = swap_pairs(send[me])
 
     def sent(e):
-        others(lambda q: remote(e, send.at[q], recv.at[e % 2, me], q).wait_send())
+        most = send.at[pl.ds(0, PEERS - 1)]
+        block_copy(e, most, most, mg, wrap(me + 1)).wait_send()
 
     def rows_of_group(g, blocks16, out, first):
         for c in range(RD // CAP):
             cols = slice(c * CAP, (c + 1) * CAP)
-            a = jnp.broadcast_to(slot[0:1, cols] // CAP - g * GROUP, (L, CAP))
+            a = jnp.concatenate([sa[:, cols] - g * GROUP] * (L // 8), axis=0)
             u = dot(blocks16, B[:, cols])
             res = out[:, cols]
             for k in range(GROUP):
@@ -154,7 +171,8 @@
 
         def one(i):
             g = lax.rem(mg + GROUPS - plane(i), GROUPS)
-            group_others(g, lambda q: arrival(e, recv.at[e % 2, q], q).wait_recv())
+            pl.when(i < GROUPS - 1)(lambda: wait_group(e, g, GROUP))
+            pl.when(i == GROUPS - 1)(lambda: wait_group(e, g, GROUP - 1))
             blk = recv[e % 2, pl.ds(g * GROUP, GROUP)].reshape(GROUP * L, CAP).astype(bf16)
             rows_of_group(g, blk, out, False)
 
@@ -190,10 +208,14 @@
     def row_to_column(x):
         return jnp.broadcast_to(x, (128, 128)).T[0:L]
 
-    def sum_start(e):
-        psend[e] = lanes_to_row(acc[...])
-        precv[e, me] = psend[e]
-        others(lambda q: remote(8 + e, psend.at[e], precv.at[e, me], q).start())
+    def sum_start():
+        psend[0] = lanes_to_row(acc[...])
+        precv[me] = psend[0]
+        send_all(5, lambda q: psend.at[0], precv.at[me])
+
+    def sum_middle():
+        wait_all(5, precv.at[pl.ds(0, PEERS - 1)])
+        sum_out(1, jnp.sum(precv[...], axis=0))
 
     def across(e, q):
         return pltpu.make_async_remote_copy(
@@ -210,20 +232,17 @@
     def other_sets(f):
         loop(SETS - 1, lambda k: f(lax.rem(st + 1 + k, SETS)))
 
-    def sum_middle(e, extra):
-        others(lambda q: arrival(8 + e, precv.at[e, q], q).wait_recv())
-        others(lambda q: remote(8 + e, psend.at[e], precv.at[e, me], q).wait_send())
-        total = jnp.sum(precv[e], axis=0)
-        if extra is not None:
-            total = total + extra
+    def sum_out(e, total):
+        total = jnp.concatenate([total, jnp.zeros((8 - total.shape[0], 128), f32)], axis=0)
         qsend[e] = total
         qrecv[e, st] = total
         other_sets(lambda q: across(e, q).start())
 
-    def sum_end(e):
+    def sum_end(e, n):
         other_sets(lambda q: across_arrival(e, q).wait_recv())
         other_sets(lambda q: across(e, q).wait_send())
-        return row_to_column(jnp.sum(qrecv[e], axis=0))
+        total = jnp.sum(qrecv[e], axis=0)
+        return [row_to_column(total[r : r + 1]) for r in range(n)]
 
     def coarse_start(e):
         g = dot_nt(d[...].astype(bf16), Cbd[...])
@@ -245,19 +264,20 @@
         for j in range(PEERS):
             gsend[e, j] = x[j * QS : (j + 1) * QS]
         grecv[e, me] = gsend[e, me]
-        others(lambda q: remote(6 + e, gsend.at[e, q], grecv.at[e, me], q).start())
+        send_all(1 + e, lambda q: gsend.at[e, q], grecv.at[e, me])
 
     def coarse_sum(e):
-        others(lambda q: arrival(6 + e, grecv.at[e, q], q).wait_recv())
-        hsend[e] = jnp.sum(grecv[e], axis=0)
+        wait_all(1 + e, grecv.at[e, pl.ds(0, PEERS - 1)])
+        hsend[e, 0:QS] = jnp.sum(grecv[e], axis=0)
+        hsend[e, QS : QS + 1] = lanes_to_row(acc[...])
+        hsend[e, QS + 1 : QS + 2] = lanes_to_row(acc0[...])
         hrecv[e, me] = hsend[e]
-        others(lambda q: remote(12 + e, hsend.at[e], hrecv.at[e, me], q).start())
-        others(lambda q: remote(6 + e, gsend.at[e, q], grecv.at[e, me], q).wait_send())
+        send_all(3 + e, lambda q: hsend.at[e], hrecv.at[e, me])
 
     def coarse_solve(e):
-        others(lambda q: arrival(12 + e, hrecv.at[e, q], q).wait_recv())
-        others(lambda q: remote(12 + e, hsend.at[e], hrecv.at[e, me], q).wait_send())
-        x = jnp.concatenate([hrecv[e, j] for j in range(PEERS)], axis=0).T
+        wait_all(3 + e, hrecv.at[e, pl.ds(0, PEERS - 1)])
+        x = jnp.concatenate([hrecv[e, j, 0:QS] for j in range(PEERS)], axis=0).T
+        sums = jnp.sum(hrecv[e, :, QS : QS + 2], axis=0)
         coarse_in = jnp.concatenate([x[q * L : (q + 1) * L] for q in range(QS)], axis=1)
         middle = jnp.dot(coarse_in, factor[...], precision=HI, preferred_element_type=f32)
         sol = lax.dot_general(
@@ -267,7 +287,8 @@
         back[...] = both[:L] + both[L:]
         kd[...] = dot(back[:, at(me, NK)].astype(bf16), Cbd[...])
         square = middle * middle
-        return lanes_to_row(sum(square[:, n * 128 : (n + 1) * 128] for n in range(NCO // 128)))
+        square = lanes_to_row(sum(square[:, n * 128 : (n + 1) * 128] for n in range(NCO // 128)))
+        sum_out(2 * e, jnp.concatenate([sums[0:1] + square, sums[1:2]], axis=0))
 
     def partners_coarse():
         def one(j):
@@ -295,6 +316,7 @@
         cols = at(c, RM)
         s = slot[0:1, cols]
         a = s // CAP
+        sa[:, cols] = jnp.broadcast_to(a, (8, RM))
         n = jnp.zeros_like(s)
         for k in range(PEERS):
             n = jnp.where(a == k, counts[0, k], n)
@@ -326,7 +348,7 @@
 
     def mask_modes(c):
         cols = at(c, CAP)
-        a = jnp.broadcast_to(slot[0:1, cols] // CAP, (NC, CAP))
+        a = sa[:, cols]
         v = crow[:, cols]
         Xm[:, cols] = jnp.concatenate(
             [jnp.where(a == k, v, 0.0) for k in range(PEERS)], axis=0
@@ -341,7 +363,7 @@
     copy_v.wait()
     gram(V)
     receive_rows(0, p)
-    others(lambda q: remote(5, csend.at[q], crecv.at[me], q).start())
+    send_all(0, lambda q: csend.at[q], crecv.at[me])
 
     def first(c):
         cols = at(c, RM)
@@ -350,11 +372,10 @@
     loop(RD // RM, first)
 
     apply(jr, V, 1.0)
-    sum_start(0)
+    acc0[...] = acc[...]
     slots_and_send(1, f)
 
-    others(lambda q: arrival(5, crecv.at[q], q).wait_recv())
-    others(lambda q: remote(5, csend.at[q], crecv.at[me], q).wait_send())
+    wait_all(0, crecv.at[pl.ds(0, PEERS - 1)])
 
     def expand(j):
         blk = crecv[j]
@@ -381,16 +402,12 @@
 
     coarse_start(0)
     apply(d, W, 2.0)
-    sum_start(1)
-    slots_and_send(2, f)
-    coarse_sum(0)
-    square = coarse_solve(0)
-    sum_middle(0, None)
-    sum_middle(1, square)
+    slots_and_send(2, f, lambda: coarse_sum(0))
+    coarse_solve(0)
     partners_coarse()
-    energy = sum_end(0)
-    alpha = energy / sum_end(1)
     receive_rows(2, p)
+    curvature, energy = sum_end(0, 2)
+    alpha = energy / curvature
 
     def update(c):
         cols = at(c, RM)
@@ -405,11 +422,11 @@
     loop(RD // RM, update)
 
     apply(jr, V, 1.0)
-    sum_start(2)
+    sum_start()
     slots_and_send(3, f)
-    sum_middle(2, None)
-    new = sum_end(2)
+    sum_middle()
     receive_rows(3, p)
+    (new,) = sum_end(1, 1)
     beta = new / energy
 
     def next_direction(c):
@@ -420,13 +437,11 @@
 
     coarse_start(1)
     apply(d, W, 2.0)
-    sum_start(3)
-    slots_and_send(4, f)
-    coarse_sum(1)
-    square = coarse_solve(1)
-    sum_middle(3, square)
-    alpha2 = new / sum_end(3)
+    slots_and_send(4, f, lambda: coarse_sum(1))
+    coarse_solve(1)
     receive_rows(4, p)
+    (curvature,) = sum_end(2, 1)
+    alpha2 = new / curvature
 
     def last(c):
         cols = at(c, RM)
@@ -461,13 +476,14 @@
             V((PEERS, L, CAP), f32), V((2, PEERS, L, CAP), f32), V((PEERS, NC, CAP), f32),
             V((PEERS, NC, CAP), f32), V((SD, NC, RM), f32), V((NC, RD), f32), V((NK, RD), bf16),
             V((PEERS, NK, CAP), bf16), V((NCO, PEERS * NK), bf16),
-            V((2, PEERS, QS, NK), f32), V((2, PEERS, QS, NK), f32), V((2, QS, NK), f32),
-            V((2, PEERS, QS, NK), f32),
+            V((2, PEERS, QS, NK), f32), V((2, PEERS, QS, NK), f32), V((2, 8, NK), f32),
+            V((2, PEERS, 8, NK), f32),
             V((L, PEERS * NK), f32), V((PEERS * L, CAP), bf16),
-            V((4, 1, 128), f32), V((4, PEERS, 1, 128), f32), V((4, 1, 128), f32),
-            V((4, SETS, 1, 128), f32), V((L, 128), f32),
-            pltpu.SemaphoreType.DMA((2,)), pltpu.SemaphoreType.DMA((14, PEERS)),
-            pltpu.SemaphoreType.DMA((14, PEERS)), pltpu.SemaphoreType.DMA((4, SETS)),
+            V((1, 1, 128), f32), V((PEERS, 1, 128), f32), V((3, 8, 128), f32),
+            V((3, SETS, 8, 128), f32), V((L, 128), f32), V((L, 128), f32), V((8, RD), jnp.int32),
+            pltpu.SemaphoreType.DMA((2,)), pltpu.SemaphoreType.DMA((5,)),
+            pltpu.SemaphoreType.DMA((5, GROUPS)), pltpu.SemaphoreType.DMA((6,)),
+            pltpu.SemaphoreType.DMA((6,)), pltpu.SemaphoreType.DMA((4, SETS)),
             pltpu.SemaphoreType.DMA((4, SETS)),
         ],
         compiler_params=pltpu.CompilerParams(

time: 177 us -> 146 us (0.82)
  Pallas kernels: 170 us -> 139 us
    pallas_call x1, Pallas kernels: 170 us -> 139 us  [body(): pl.pallas_call(kernel, out_shape=(jax.ShapeDtypeStruct((L, RD), f32),) *...]
where the time goes in v3:
time: 146 us
  Pallas kernels  139 us (95%)
  local copies, waits for them, and re-layouts  5.22 us (4%)
    pallas_call x1, Pallas kernels, body(): pl.pallas_call(kernel, out_shape=(jax.ShapeDtypeStruct((L, RD), f32),) *...  139 us
    unnamed x3, local copies, waits for them, and re-layouts  4.61 us

profile of v3, /device:TPU:1, one launch (start us, length us, event | category | flops | bytes accessed | tf_op | source)
XLA Modules:
  0.0 145.8 jit_solution(3231728097462773840)
XLA Ops:
  0.6 0.7 convert_element_type.3
  1.3 0.1 copy.12
  1.4 0.6 reshape.11.corner
  2.0 139.3 %shard_map.95 = (f32[32,8192]{1,0:T(8,128)}, f32[32,8192]{1,0:T(8,128)}) custom-call(f32[32,8192]{1,0:T(8,128)} %jump.1, bf16[16,512,512]{2,1,0:T(8,128)(2,1)} %w_hbm.1, bf16[16,512,512]{2,1,0:T(8,128)(2,1)} %s_hbm.1, f32[6,16,512]{2,1,0:T(8,128)} %bitcast.2, f32[512,512]{1,0:T(8,128)} %factor.1, s32[1,8192]{1,0:T(1,128)} %bitcast.3, s32[1,32]{1,0:T(1,128)} %counts.1, ...), custom_call_target="tpu_custom_call" | custom-call | flops 60000002048 | bytes 20971520 | tf_op jit(solution)/shard_map/pallas_call | solution.py:468
  141.3 2.3 %copy.15 = f32[32,8192]{1,0:T(8,128)} copy(f32[32,8192]{1,0:T(8,128)} %get-tuple-element.4) | data formatting | bytes 2097152
  143.5 2.3 %copy.16 = f32[32,8192]{1,0:T(8,128)} copy(f32[32,8192]{1,0:T(8,128)} %get-tuple-element.5) | data formatting | bytes 2097152
  (1 shorter events, 0.0 us)

commit v4 on v3

--- a/solution.py
+++ b/solution.py
@@ -120,10 +120,10 @@
 
             @pl.when(q != me)
             def _():
-                block_copy(e, send.at[q], recv.at[e % 2, me], mg, q).start()
+                block_copy(e, send.at[q], recv.at[e % 3, me], mg, q).start()
 
     def wait_group(e, g, n):
-        some = recv.at[e % 2, pl.ds(g * GROUP, n)]
+        some = recv.at[e % 3, pl.ds(g * GROUP, n)]
         block_copy(e, some, some, g, wrap(me + 1)).wait_recv()
 
     def plane(i):
@@ -150,7 +150,7 @@
             send_group(e, g)
 
         loop(GROUPS, one)
-        recv[e % 2, me] = swap_pairs(send[me])
+        recv[e % 3, me] = swap_pairs(send[me])
 
     def sent(e):
         most = send.at[pl.ds(0, PEERS - 1)]
@@ -166,25 +166,38 @@
                 res = jnp.where(a == k, u[k * L : (k + 1) * L], res)
             out[:, cols] = res
 
-    def receive_rows(e, out):
+    def receive_rows(e, out, change=None):
         out[...] = jnp.zeros_like(out)
 
         def one(i):
             g = lax.rem(mg + GROUPS - plane(i), GROUPS)
             pl.when(i < GROUPS - 1)(lambda: wait_group(e, g, GROUP))
             pl.when(i == GROUPS - 1)(lambda: wait_group(e, g, GROUP - 1))
-            blk = recv[e % 2, pl.ds(g * GROUP, GROUP)].reshape(GROUP * L, CAP).astype(bf16)
-            rows_of_group(g, blk, out, False)
+            blk = recv[e % 3, pl.ds(g * GROUP, GROUP)].reshape(GROUP * L, CAP)
+            if change is not None:
+                blk = change(blk, g)
+            rows_of_group(g, blk.astype(bf16), out, False)
 
         loop(GROUPS, one)
-        sent(e)
+        most = send.at[pl.ds(0, PEERS - 1)]
+        block_copy(e, most, most, mg, wrap(me + 1)).wait_send()
+
+    def rows_again(e, out):
+        out[...] = jnp.zeros_like(out)
+
+        def one(g):
+            blk = recv[e % 3, pl.ds(g * GROUP, GROUP)].reshape(GROUP * L, CAP)
+            rows_of_group(g, blk.astype(bf16), out, False)
+
+        loop(GROUPS, one)
 
     def gram(F):
-        def one(s):
-            m = F[s]
-            F[s] = dot_nt(m, m).astype(bf16)
-
-        loop(SD, one)
+        def one(i):
+            for k in range(4):
+                m = F[i * 4 + k]
+                F[i * 4 + k] = dot_nt(m, m).astype(bf16)
+
+        loop(SD // 4, one)
 
     def apply(x, F, scale):
         acc[...] = jnp.zeros_like(acc)
@@ -292,16 +305,11 @@
 
     def partners_coarse():
         def one(j):
-            pks[pl.ds(pl.multiple_of(j * L, L), L), :] = dot(
-                back[:, at(j, NK)].astype(bf16), Ce[j]
-            ).astype(bf16)
-
-        loop(PEERS, one)
-        pk[...] = jnp.zeros_like(pk)
-        loop(
-            GROUPS,
-            lambda g: rows_of_group(g, pks[at(g, GROUP * L), :], pk, False),
-        )
+            for k in range(4):
+                q = j * 4 + k
+                pks[at(q, L), :] = dot(back[:, at(q, NK)].astype(bf16), Ce[q])
+
+        loop(PEERS // 4, one)
 
     def onehot(c):
         cols = at(c, CAP)
@@ -405,7 +413,7 @@
     slots_and_send(2, f, lambda: coarse_sum(0))
     coarse_solve(0)
     partners_coarse()
-    receive_rows(2, p)
+    receive_rows(2, p, lambda blk, g: 2.0 * blk + pks[at(g, GROUP * L), :])
     curvature, energy = sum_end(0, 2)
     alpha = energy / curvature
 
@@ -413,11 +421,10 @@
         cols = at(c, RM)
         on = live[0:1, cols]
         al = alpha[:, 0:1]
-        jf = f[:, cols] + p[:, cols]
-        k = kd[:, cols]
+        part = f[:, cols] + kd[:, cols]
         mult[:, cols] = al * d[:, cols]
-        resid[:, cols] -= al * (on * (jf + k))
-        jr[:, cols] -= al * (on * (2.0 * jf + k + pk[:, cols]))
+        resid[:, cols] -= al * (on * part)
+        jr[:, cols] -= al * (on * (part + f[:, cols] + p[:, cols]))
 
     loop(RD // RM, update)
 
@@ -425,13 +432,16 @@
     sum_start()
     slots_and_send(3, f)
     sum_middle()
+    rows_again(2, pk)
     receive_rows(3, p)
     (new,) = sum_end(1, 1)
     beta = new / energy
 
     def next_direction(c):
         cols = at(c, RM)
-        d[:, cols] = live[0:1, cols] * (f[:, cols] + p[:, cols]) + beta[:, 0:1] * d[:, cols]
+        on = live[0:1, cols]
+        resid[:, cols] -= alpha[:, 0:1] * (on * pk[:, cols])
+        d[:, cols] = on * (f[:, cols] + p[:, cols]) + beta[:, 0:1] * d[:, cols]
 
     loop(RD // RM, next_direction)
 
@@ -450,6 +460,23 @@
         resid[:, cols] -= al * (live[0:1, cols] * (f[:, cols] + p[:, cols] + kd[:, cols]))
 
     loop(RD // RM, last)
+
+
+def hand_on(a, b, a_out, b_out, buf, sem_in, sem_out):
+    pairs = [
+        (n * (L // 8) + k, x.at[8 * k : 8 * k + 8], y.at[8 * k : 8 * k + 8])
+        for n, (x, y) in enumerate(((a, a_out), (b, b_out)))
+        for k in range(L // 8)
+    ]
+    first = [pltpu.make_async_copy(x, buf.at[i], sem_in.at[i]) for i, x, _ in pairs]
+    second = [pltpu.make_async_copy(buf.at[i], y, sem_out.at[i]) for i, _, y in pairs]
+    for copy in first:
+        copy.start()
+    for one, two in zip(first, second):
+        one.wait()
+        two.start()
+    for copy in second:
+        copy.wait()
 
 
 def body(
@@ -465,7 +492,7 @@
     sm = pl.BlockSpec(memory_space=pltpu.SMEM)
     V = pltpu.VMEM
     vec = V((L, RD), f32)
-    return pl.pallas_call(
+    results = pl.pallas_call(
         kernel,
         out_shape=(jax.ShapeDtypeStruct((L, RD), f32),) * 2,
         in_specs=[vm, hbm, hbm, vm, vm, vm, sm, vm],
@@ -473,12 +500,12 @@
         scratch_shapes=[
             V((SD, RM, RM), bf16), V((SD, RM, RM), bf16), V((CAP, RD), bf16), V((RD, CAP), bf16),
             V((GROUP * L, RD), bf16), V((8, RD), f32), vec, vec, vec, vec, vec, vec,
-            V((PEERS, L, CAP), f32), V((2, PEERS, L, CAP), f32), V((PEERS, NC, CAP), f32),
+            V((PEERS, L, CAP), f32), V((3, PEERS, L, CAP), f32), V((PEERS, NC, CAP), f32),
             V((PEERS, NC, CAP), f32), V((SD, NC, RM), f32), V((NC, RD), f32), V((NK, RD), bf16),
             V((PEERS, NK, CAP), bf16), V((NCO, PEERS * NK), bf16),
             V((2, PEERS, QS, NK), f32), V((2, PEERS, QS, NK), f32), V((2, 8, NK), f32),
             V((2, PEERS, 8, NK), f32),
-            V((L, PEERS * NK), f32), V((PEERS * L, CAP), bf16),
+            V((L, PEERS * NK), f32), V((PEERS * L, CAP), f32),
             V((1, 1, 128), f32), V((PEERS, 1, 128), f32), V((3, 8, 128), f32),
             V((3, SETS, 8, 128), f32), V((L, 128), f32), V((L, 128), f32), V((8, RD), jnp.int32),
             pltpu.SemaphoreType.DMA((2,)), pltpu.SemaphoreType.DMA((5,)),
@@ -493,6 +520,16 @@
             flops=60_000_000_000, bytes_accessed=20 << 20, transcendentals=0
         ),
     )(jump_rhs, w_factor, s_factor, rigid_coarse_blocks, coarse_factor, slot, pair_counts, corner)
+    return pl.pallas_call(
+        hand_on,
+        out_shape=(jax.ShapeDtypeStruct((L, RD), f32),) * 2,
+        in_specs=[hbm, hbm],
+        out_specs=[hbm, hbm],
+        scratch_shapes=[
+            V((L // 4, 8, RD), f32), pltpu.SemaphoreType.DMA((L // 4,)),
+            pltpu.SemaphoreType.DMA((L // 4,)),
+        ],
+    )(*results)
 
 
 def solution(mesh):

time: 146 us -> 138 us (0.945)
  local copies, waits for them, and re-layouts: 5.22 us -> 0.7 us
  Pallas kernels: 139 us -> 135 us
    pallas_call x1, Pallas kernels: 139 us -> 133 us  [body(): pl.pallas_call(kernel, out_shape=(jax.ShapeDtypeStruct((L, RD), f32),) *...]
    unnamed x3 -> x1, local copies, waits for them, and re-layouts: 4.61 us -> 0.09 us
    pallas_call x0 -> x1, Pallas kernels: none -> 2.4 us  [body(): pl.pallas_call(hand_on, out_shape=(jax.ShapeDtypeStruct((L, RD), f32),) *...]
where the time goes in v4:
time: 138 us; the launch traced here: 137 us
  Pallas kernels  135 us (98%)
    pallas_call x1, Pallas kernels, body(): pl.pallas_call(kernel, out_shape=(jax.ShapeDtypeStruct((L, RD), f32),) *...  133 us

profile of v4, /device:TPU:1, one launch (start us, length us, event | category | flops | bytes accessed | tf_op | source)
XLA Modules:
  0.0 137.3 jit_solution(2934392670524005267)
XLA Ops:
  0.6 0.7 convert_element_type.3
  1.3 0.1 copy.12
  1.4 0.6 reshape.11.corner
  2.0 132.7 %shard_map.95 = (f32[32,8192]{1,0:T(8,128)}, f32[32,8192]{1,0:T(8,128)}) custom-call(f32[32,8192]{1,0:T(8,128)} %jump.1, bf16[16,512,512]{2,1,0:T(8,128)(2,1)} %w_hbm.1, bf16[16,512,512]{2,1,0:T(8,128)(2,1)} %s_hbm.1, f32[6,16,512]{2,1,0:T(8,128)} %bitcast.2, f32[512,512]{1,0:T(8,128)} %factor.1, s32[1,8192]{1,0:T(1,128)} %bitcast.3, s32[1,32]{1,0:T(1,128)} %counts.1, ...), custom_call_target="tpu_custom_call" | custom-call | flops 60000002048 | bytes 20971520 | tf_op jit(solution)/shard_map/pallas_call | solution.py:495
  134.7 2.4 %shard_map.96 = (f32[32,8192]{1,0:T(8,128)}, f32[32,8192]{1,0:T(8,128)}) custom-call(f32[32,8192]{1,0:T(8,128)} %get-tuple-element.4.a, f32[32,8192]{1,0:T(8,128)} %get-tuple-element.5.b), custom_call_target="tpu_custom_call" | custom-call | tf_op jit(solution)/shard_map/pallas_call | solution.py:523
  (1 shorter events, 0.0 us)

commit v5 on v4

--- a/solution.py
+++ b/solution.py
@@ -53,12 +53,12 @@
 
 
 def kernel(
-    jump, w_hbm, s_hbm, blocks, factor, slot, counts, corner,
+    jump, w_hbm, s_hbm, blocks, factor, slot, counts, corners,
     mult, resid,
     W, V, B, BT, Xm, live, jr, f, p, d, kd, pk,
     send, recv, csend, crecv, cpad, crow, Cbd, Ce, OHT,
     gsend, grecv, hsend, hrecv, back, pks, psend, precv, qsend, qrecv, acc, acc0,
-    sa, wsem, assem, arsem, ssem, rsem, qssem, qrsem,
+    sa, corner, wsem, assem, arsem, ssem, rsem, qssem, qrsem,
 ):
     st = lax.axis_index("set")
     me = lax.axis_index("sub")
@@ -333,6 +333,13 @@
         resid[:, cols] = on * jump[:, cols]
 
     loop(RD // RM, live_rows)
+
+    place = lax.broadcasted_iota(jnp.int32, (1, NK), 1)
+    unknown = jnp.full((1, NK), -1, jnp.int32)
+    for s in range(SD):
+        for k in range(6):
+            unknown = jnp.where(place == s * NC + k, corners[k, s], unknown)
+    corner[...] = unknown.astype(f32)
 
     cpad[...] = jnp.zeros_like(cpad)
     for s in range(SD):
@@ -484,8 +491,7 @@
     corner_map,
 ):
     slot = slot_of_row.reshape(1, RD)
-    corner = jnp.pad(corner_map.astype(f32), ((0, 0), (0, 2)), constant_values=-1.0)
-    corner = corner.reshape(1, NK)
+    corners = jnp.transpose(corner_map)
     rigid_coarse_blocks = jnp.transpose(rigid_coarse_blocks, (1, 0, 2))
     vm = pl.BlockSpec(memory_space=pltpu.VMEM)
     hbm = pl.BlockSpec(memory_space=pl.ANY)
@@ -495,7 +501,7 @@
     results = pl.pallas_call(
         kernel,
         out_shape=(jax.ShapeDtypeStruct((L, RD), f32),) * 2,
-        in_specs=[vm, hbm, hbm, vm, vm, vm, sm, vm],
+        in_specs=[vm, hbm, hbm, vm, vm, vm, sm, sm],
         out_specs=[vm, vm],
         scratch_shapes=[
             V((SD, RM, RM), bf16), V((SD, RM, RM), bf16), V((CAP, RD), bf16), V((RD, CAP), bf16),
@@ -507,7 +513,7 @@
             V((2, PEERS, 8, NK), f32),
             V((L, PEERS * NK), f32), V((PEERS * L, CAP), f32),
             V((1, 1, 128), f32), V((PEERS, 1, 128), f32), V((3, 8, 128), f32),
-            V((3, SETS, 8, 128), f32), V((L, 128), f32), V((L, 128), f32), V((8, RD), jnp.int32),
+            V((3, SETS, 8, 128), f32), V((L, 128), f32), V((L, 128), f32), V((8, RD), jnp.int32), V((1, NK), f32),
             pltpu.SemaphoreType.DMA((2,)), pltpu.SemaphoreType.DMA((5,)),
             pltpu.SemaphoreType.DMA((5, GROUPS)), pltpu.SemaphoreType.DMA((6,)),
             pltpu.SemaphoreType.DMA((6,)), pltpu.SemaphoreType.DMA((4, SETS)),
@@ -519,7 +525,7 @@
         cost_estimate=pl.CostEstimate(
             flops=60_000_000_000, bytes_accessed=20 << 20, transcendentals=0
         ),
-    )(jump_rhs, w_factor, s_factor, rigid_coarse_blocks, coarse_factor, slot, pair_counts, corner)
+    )(jump_rhs, w_factor, s_factor, rigid_coarse_blocks, coarse_factor, slot, pair_counts, corners)
     return pl.pallas_call(
         hand_on,
         out_shape=(jax.ShapeDtypeStruct((L, RD), f32),) * 2,

time: 138 us -> 137 us (level)
  no operation moved by 1% of the time
where the time goes in v5:
time: 137 us; the launch traced here: 136 us
  Pallas kernels  135 us (99%)
    pallas_call x1, Pallas kernels, body(): pl.pallas_call(kernel, out_shape=(jax.ShapeDtypeStruct((L, RD), f32),) *...  132 us

profile of v5, /device:TPU:1, one launch (start us, length us, event | category | flops | bytes accessed | tf_op | source)
XLA Modules:
  0.0 135.5 jit_solution(10924174578547952202)
XLA Ops:
  0.6 132.3 %shard_map.95 = (f32[32,8192]{1,0:T(8,128)}, f32[32,8192]{1,0:T(8,128)}) custom-call(f32[32,8192]{1,0:T(8,128)} %jump.1, bf16[16,512,512]{2,1,0:T(8,128)(2,1)} %w_hbm.1, bf16[16,512,512]{2,1,0:T(8,128)(2,1)} %s_hbm.1, f32[6,16,512]{2,1,0:T(8,128)} %bitcast.3, f32[512,512]{1,0:T(8,128)} %factor.1, s32[1,8192]{1,0:T(1,128)} %bitcast.4, s32[1,32]{1,0:T(1,128)} %counts.1, ...), custom_call_target="tpu_custom_call" | custom-call | flops 60000002048 | bytes 20971520 | tf_op jit(solution)/shard_map/pallas_call | solution.py:501
  132.9 2.4 %shard_map.96 = (f32[32,8192]{1,0:T(8,128)}, f32[32,8192]{1,0:T(8,128)}) custom-call(f32[32,8192]{1,0:T(8,128)} %get-tuple-element.4.a, f32[32,8192]{1,0:T(8,128)} %get-tuple-element.5.b), custom_call_target="tpu_custom_call" | custom-call | tf_op jit(solution)/shard_map/pallas_call | solution.py:529
